TPU v7x, 512 devices: a whole 4x8x8 slice. The times are simulated.
512 devices in a mesh: prompt: 16 (over x, z_hi), resp: 32 (over z_lo, y, core).
Axes of the slice: x: 4, y: 8, z: 8 (z_hi: 4, z_lo: 2; z = z_hi * 2 + z_lo), core: 2. Of those that a mesh axis runs over, the one named last changes fastest.
Arguments:
- query: bfloat16 [512, 256, 2048], P(('prompt', 'resp')), may hold values from -6 to 6
- resp_keys: bfloat16 [512, 256, 512], P(('prompt', 'resp')), may hold values from -6 to 6
- resp_values: bfloat16 [512, 256, 512], P(('prompt', 'resp')), may hold values from -6 to 6
- prompt_keys: bfloat16 [8, 128, 512], P(None, 'prompt'), may hold values from -6 to 6
- prompt_values: bfloat16 [8, 128, 512], P(None, 'prompt'), may hold values from -6 to 6
- out_grad: bfloat16 [512, 256, 2048], P(('prompt', 'resp')), may hold values from -6 to 6
- group: int32 [512], replicated, may hold values from 0 to 7
- lengths: int32 [512], P(('prompt', 'resp')), may hold values from 1 to 256, 81920 in all
Outputs:
- query_grad: bfloat16 [512, 256, 2048], P(('prompt', 'resp'))
- resp_key_grad: bfloat16 [512, 256, 512], P(('prompt', 'resp'))
- resp_value_grad: bfloat16 [512, 256, 512], P(('prompt', 'resp'))
- prompt_key_grad: float32 [8, 128, 512], P(None, 'prompt')
- prompt_value_grad: float32 [8, 128, 512], P(None, 'prompt')
Inputs may be any that keep to these rules, and one draw needn't show every extreme that they name: `group`: response r stands on device r of prompt+resp, in the mesh's order. `lengths`: a response's live tokens come first; some response fills all 256 slots.
All inputs are finite; a program needn't handle non-finite values. No bound on the sum of `lengths` on one device may be relied on, other than what follows from the above.
Results may differ from a plain program's by a relative error of at most 0.0097.
Values may be sent and summed in bfloat16 or wider, within the bound.
No kernel may reach another device: no remote copies, remote signals or barrier semaphores. Data moves between devices by JAX's collectives and lax.ppermute only.
A program may use at most 64 MiB of HBM per device.

v0:
```python
import math

import jax
import jax.numpy as jnp
from jax import lax
from jax.sharding import PartitionSpec as P

QH = 16
KVH = 4
HD = 128


masked_score = -1e30


def attend_backward(query_rows, grad_rows, all_keys, all_values, length, front_len):
    resp_len = query_rows.shape[0]
    total_len = all_keys.shape[0]
    score_scale = 1.0 / math.sqrt(HD)
    row_ids = jnp.arange(resp_len)[:, None]
    col_ids = jnp.arange(total_len)[None, :]
    allowed = (col_ids < front_len) | (col_ids - front_len <= row_ids)
    live_rows = (jnp.arange(resp_len) < length)[:, None]
    grad_rows = jnp.where(live_rows, grad_rows, jnp.zeros_like(grad_rows))
    group_size = QH // KVH
    query_four = query_rows.reshape(resp_len, KVH, group_size, HD)
    grad_four = grad_rows.reshape(resp_len, KVH, group_size, HD)
    query_parts = []
    key_parts = []
    value_parts = []
    for kv_head in range(KVH):
        head_keys = all_keys[:, kv_head * HD : (kv_head + 1) * HD]
        head_values = all_values[:, kv_head * HD : (kv_head + 1) * HD]
        head_query = query_four[:, kv_head]
        head_grad = grad_four[:, kv_head]
        scores = (
            jnp.einsum("igd,jd->gij", head_query, head_keys, preferred_element_type=jnp.float32)
            * score_scale
        )
        scores = jnp.where(allowed[None], scores, masked_score)
        row_max = jnp.max(scores, -1, keepdims=True)
        weights = jnp.where(allowed[None], jnp.exp(scores - row_max), 0.0)
        attn_prob = weights / jnp.sum(weights, -1, keepdims=True)
        prob_low = attn_prob.astype(jnp.bfloat16)
        attn_out = jnp.einsum(
            "gij,jd->igd", prob_low, head_values, preferred_element_type=jnp.float32
        )
        delta = jnp.transpose(jnp.sum(head_grad.astype(jnp.float32) * attn_out, -1))
        dprob = jnp.einsum(
            "igd,jd->gij", head_grad, head_values, preferred_element_type=jnp.float32
        )
        dscore_low = (attn_prob * (dprob - delta[:, :, None])).astype(jnp.bfloat16)
        query_term = (
            jnp.einsum("gij,jd->igd", dscore_low, head_keys, preferred_element_type=jnp.float32)
            * score_scale
        )
        key_term = (
            jnp.einsum("gij,igd->jd", dscore_low, head_query, preferred_element_type=jnp.float32)
            * score_scale
        )
        value_term = jnp.einsum(
            "gij,igd->jd", prob_low, head_grad, preferred_element_type=jnp.float32
        )
        query_parts.append(query_term.reshape(resp_len, group_size * HD))
        key_parts.append(key_term)
        value_parts.append(value_term)
    query_grad = jnp.concatenate(query_parts, -1).astype(jnp.bfloat16)
    return (query_grad, jnp.concatenate(key_parts, -1), jnp.concatenate(value_parts, -1))


def shards(query, resp_keys, resp_values, prompt_keys, prompt_values, out_grad, group, lengths):
    resp_count = lax.axis_size("resp")
    prompt_index = lax.axis_index("prompt")
    resp_index = lax.axis_index("resp")
    my_prompt = lax.dynamic_index_in_dim(
        group, prompt_index * resp_count + resp_index, 0, keepdims=False
    )
    num_prompts = prompt_keys.shape[0]
    prompt_ids = jnp.arange(num_prompts)
    every_keys, every_values = (
        lax.all_gather(prompt_keys, "prompt", axis=1, tiled=True),
        lax.all_gather(prompt_values, "prompt", axis=1, tiled=True),
    )
    front_keys = lax.dynamic_index_in_dim(every_keys, my_prompt, 0, keepdims=False)
    front_values = lax.dynamic_index_in_dim(every_values, my_prompt, 0, keepdims=False)
    front_len = front_keys.shape[0]
    all_keys = jnp.concatenate([front_keys, resp_keys[0]], 0)
    all_values = jnp.concatenate([front_values, resp_values[0]], 0)
    query_grad, key_all, value_all = attend_backward(
        query[0], out_grad[0], all_keys, all_values, lengths[0], front_len
    )
    prompt_key_term = key_all[:front_len]
    prompt_value_term = value_all[:front_len]
    hit_mask = (prompt_ids == my_prompt)[:, None, None]
    spread_keys = jnp.where(hit_mask, prompt_key_term[None], 0.0)
    spread_values = jnp.where(hit_mask, prompt_value_term[None], 0.0)
    local_keys, local_values = (
        lax.psum_scatter(spread_keys, "prompt", scatter_dimension=1, tiled=True),
        lax.psum_scatter(spread_values, "prompt", scatter_dimension=1, tiled=True),
    )
    prompt_key_grad, prompt_value_grad = lax.psum((local_keys, local_values), "resp")
    return (
        query_grad[None],
        key_all[front_len:].astype(jnp.bfloat16)[None],
        value_all[front_len:].astype(jnp.bfloat16)[None],
        prompt_key_grad,
        prompt_value_grad,
    )


def solution(mesh):
    return jax.shard_map(
        shards,
        mesh=mesh,
        in_specs=(
            P(("prompt", "resp"), None, None),
            P(("prompt", "resp"), None, None),
            P(("prompt", "resp"), None, None),
            P(None, "prompt", None),
            P(None, "prompt", None),
            P(("prompt", "resp"), None, None),
            P(),
            P(("prompt", "resp")),
        ),
        out_specs=(
            P(("prompt", "resp"), None, None),
            P(("prompt", "resp"), None, None),
            P(("prompt", "resp"), None, None),
            P(None, "prompt", None),
            P(None, "prompt", None),
        ),
        check_vma=False,
    )
```

profile of v0, /device:TPU:1, one launch (start us, length us, event | category | flops | bytes accessed | tf_op | source)
XLA Modules:
  0.0 594.2 jit_solution(14031072275264456639)
XLA Ops:
  7.2 0.7 all-gather.5.cloned.1.call-update
  8.0 0.7 all-gather.3.cloned.1.call-update
  9.4 1.3 dynamic_slice.11
  11.9 1.5 copy.57
  13.4 0.5 copy.59
  14.0 0.7 copy.60
  15.3 0.7 iota_compare_fusion.3
  16.4 60.2 %all-gather.5.cloned.1.call-done = bf16[8,128,512]{2,1,0:T(8,128)(2,1)} async-done(((bf16[8,8,512]{2,1,0:T(8,128)(2,1)}), bf16[8,128,512]{2,1,0:T(8,128)(2,1)}) %all-gather.5.cloned.1.call-update) | async-done | bytes 1048592 | tf_op jit(solution)/shard_map/all_gather | solution.py:82
  76.6 0.9 dynamic-slice_bitcast_fusion
  77.5 59.2 %all-gather.3.cloned.1.call-done = bf16[8,128,512]{2,1,0:T(8,128)(2,1)} async-done(((bf16[8,8,512]{2,1,0:T(8,128)(2,1)}), bf16[8,128,512]{2,1,0:T(8,128)(2,1)}) %all-gather.3.cloned.1.call-update) | async-done | bytes 1048592 | tf_op jit(solution)/shard_map/all_gather | solution.py:81
  136.7 0.9 dynamic-slice_bitcast_fusion.1
  137.7 0.9 fusion.52
  138.5 2.8 fusion.90
  141.3 1.5 fusion.34
  142.8 0.6 fusion.26
  143.5 1.1 convolution_bitcast_fusion.5
  144.5 1.9 fusion.93
  146.5 1.5 fusion.33
  148.0 0.6 fusion.25
  148.6 1.1 convolution_bitcast_fusion.6
  149.7 1.9 fusion.96
  151.6 1.5 fusion.32
  153.1 0.6 fusion.24
  153.8 1.1 convolution_bitcast_fusion.7
  155.2 1.1 fusion.29
  156.8 1.0 fusion.30
  158.4 0.9 copy-done.6
  159.3 1.0 fusion.31
  160.3 1.9 fusion.89
  162.3 1.5 fusion.35
  163.8 1.0 convolution_bitcast_fusion.4
  164.8 0.6 fusion.27
  165.5 1.3 fusion.9
  168.2 2.7 broadcast_select_fusion
  171.0 0.5 reduce-scatter.3.cloned.1.call-update
  172.0 1.8 pad_maximum_fusion.2
  173.8 0.7 fusion.37
  174.5 1.0 fusion.22
  175.6 1.0 fusion.21
  176.6 1.0 fusion.20
  178.0 83.6 %reduce-scatter.5.cloned.1.call-done = f32[8,8,512]{2,1,0:T(8,128)} async-done(((f32[8,128,512]{2,1,0:T(8,128)}), f32[8,8,512]{2,1,0:T(8,128)}) %reduce-scatter.5.cloned.1.call-update) | async-done | bytes 131088 | tf_op jit(solution)/shard_map/reduce_scatter | solution.py:99
  261.6 96.4 %reduce-scatter.3.cloned.1.call-done = f32[8,8,512]{2,1,0:T(8,128)} async-done(((f32[8,128,512]{2,1,0:T(8,128)}), f32[8,8,512]{2,1,0:T(8,128)}) %reduce-scatter.3.cloned.1.call-update) | async-done | bytes 131088 | tf_op jit(solution)/shard_map/reduce_scatter | solution.py:98
  358.8 0.8 copy.106
  359.6 0.8 copy.107
  360.5 1.1 pad_maximum_fusion
  361.6 222.9 %all-reduce.3.cloned.1.call-done = (f32[8,8,512]{2,1,0:T(8,128)}, f32[8,8,512]{2,1,0:T(8,128)}) async-done(((f32[8,8,512]{2,1,0:T(8,128)}, f32[8,8,512]{2,1,0:T(8,128)}), (f32[8,8,512]{2,1,0:T(8,128)}, f32[8,8,512]{2,1,0:T(8,128)})) %all-reduce.3.cloned.1.call-update) | async-done | bytes 262160 | tf_op jit(solution)/shard_map/psum | solution.py:101
  584.5 1.6 copy.159
  586.1 1.6 copy.160
  (87 shorter events, 4.7 us)
Async XLA Ops:
  7.2 6.2 %copy-start.22 = (bf16[1,256,2048]{2,1,0:T(8,128)(2,1)S(1)}, bf16[1,256,2048]{2,1,0:T(8,128)(2,1)}, u32[]{:S(2)}) copy-start(bf16[1,256,2048]{2,1,0:T(8,128)(2,1)} %param.13) | copy-start | bytes 3145732
  7.2 69.4 %all-gather.5.cloned.1.call-start = ((), (), s32[]{:S(2)}) async-start(), calls=%async_computation.3 | async-start | bytes 1114112 | tf_op jit(solution)/shard_map/all_gather | solution.py:82
  7.9 128.8 %all-gather.3.cloned.1.call-start = ((), (), s32[]{:S(2)}) async-start(), calls=%async_computation.2 | async-start | bytes 1114112 | tf_op jit(solution)/shard_map/all_gather | solution.py:81
  8.7 253.0 %reduce-scatter.5.cloned.1.call-start = ((), (), s32[]{:S(2)}) async-start(), calls=%async_computation.5 | async-start | bytes 2228224 | tf_op jit(solution)/shard_map/reduce_scatter | solution.py:99
  14.6 62.9 %copy-start = (bf16[1,256,512]{2,1,0:T(8,128)(2,1)S(1)}, bf16[1,256,512]{2,1,0:T(8,128)(2,1)}, u32[]{:S(2)}) copy-start(bf16[1,256,512]{2,1,0:T(8,128)(2,1)} %param.10) | copy-start | bytes 786436
  77.5 87.3 %copy-start.29 = (bf16[384,128,1]{1,0,2:T(8,128)(2,1)}, bf16[384,128,1]{1,0,2:T(8,128)(2,1)S(1)}, u32[]{:S(2)}) copy-start(bf16[384,128,1]{1,0,2:T(8,128)(2,1)S(1)} %fusion.51) | copy-start | bytes 294916
  138.5 21.8 %copy-start.27 = (bf16[384,128,1]{1,0,2:T(8,128)(2,1)}, bf16[384,128,1]{1,0,2:T(8,128)(2,1)S(1)}, u32[]{:S(2)}) copy-start(bf16[384,128,1]{1,0,2:T(8,128)(2,1)S(1)} %fusion.52) | copy-start | bytes 294916
  142.8 1.7 copy-start.1
  153.1 1.7 copy-start.17
  154.8 1.6 copy-start.18
  155.2 1.6 copy-start.2
  156.4 1.6 copy-start.19
  156.8 1.6 copy-start.4
  158.4 0.9 copy-start.6
  163.8 1.7 copy-start.20
  165.5 1.8 copy-start.11
  165.5 1.8 copy-start.12
  165.5 1.8 copy-start.14
  166.8 0.9 copy-start.8
  166.9 1.0 copy-start.9
  166.9 1.1 copy-start.10
  166.9 1.2 copy-start.16
  170.9 0.9 copy-start.13
  170.9 1.0 copy-start.15
  170.9 187.2 %reduce-scatter.3.cloned.1.call-start = ((), (), s32[]{:S(2)}) async-start(), calls=%async_computation.4 | async-start | bytes 2228224 | tf_op jit(solution)/shard_map/reduce_scatter | solution.py:98
  171.5 3.0 copy-start.3
  171.5 413.0 %all-reduce.3.cloned.1.call-start = ((), (), s32[]{:S(2)}) async-start(), calls=%async_computation.6 | async-start | bytes 524288 | tf_op jit(solution)/shard_map/psum | solution.py:101
  172.0 3.6 copy-start.5
  174.5 2.1 copy-start.7
  175.6 2.1 copy-start.28
  176.6 181.5 %copy-start.21 = (bf16[384,512]{0,1:T(8,128)(2,1)S(1)}, bf16[384,512]{0,1:T(8,128)(2,1)}, u32[]{:S(2)}) copy-start(bf16[384,512]{0,1:T(8,128)(2,1)} %pad_maximum_fusion.2) | copy-start | bytes 1179652
  176.6 181.5 %copy-start.24 = (bf16[128,4,256]{2,0,1:T(8,128)(2,1)S(1)}, bf16[128,4,256]{2,0,1:T(8,128)(2,1)}, u32[]{:S(2)}) copy-start(bf16[128,4,256]{2,0,1:T(8,128)(2,1)} %fusion.22) | copy-start | bytes 786436
  177.7 180.7 %copy-start.25 = (bf16[128,4,256]{2,0,1:T(8,128)(2,1)S(1)}, bf16[128,4,256]{2,0,1:T(8,128)(2,1)}, u32[]{:S(2)}) copy-start(bf16[128,4,256]{2,0,1:T(8,128)(2,1)} %fusion.21) | copy-start | bytes 786436
  177.7 180.8 %copy-start.26 = (bf16[128,4,256]{2,0,1:T(8,128)(2,1)S(1)}, bf16[128,4,256]{2,0,1:T(8,128)(2,1)}, u32[]{:S(2)}) copy-start(bf16[128,4,256]{2,0,1:T(8,128)(2,1)} %fusion.20) | copy-start | bytes 786436
  178.0 180.8 %copy-start.23 = (bf16[1,256,512]{1,2,0:T(8,128)(2,1)S(1)}, bf16[1,256,512]{1,2,0:T(8,128)(2,1)}, u32[]{:S(2)}) copy-start(bf16[1,256,512]{1,2,0:T(8,128)(2,1)} %fusion.37) | copy-start | bytes 786436
Sparse Core Ops, SparseCore 0:
  11.0 65.5 all-gather.4
  79.6 57.1 all-gather.2
  171.0 90.5 reduce-scatter.4
  266.2 91.8 reduce-scatter.2
  360.9 223.5 all-reduce.2
where the time goes:
time: 595 us; the launch traced here: 594 us
  waiting for transfers between devices  524 us (88%)
  matrix products  24.6 us (4%)
  between operations  16.9 us (3%)
  local copies, waits for them, and re-layouts  14.4 us (2%)
  other arithmetic  13.7 us (2%)
    psum x1, waiting for transfers between devices, shards(): lax.psum((local_keys, local_values), 'resp')  223 us
    reduce_scatter x1, waiting for transfers between devices, shards(): lax.psum_scatter(spread_keys, 'prompt', scatter_dimension=1, tiled=True)  96.4 us
    reduce_scatter x1, waiting for transfers between devices, shards(): lax.psum_scatter(spread_values, 'prompt', scatter_dimension=1, tiled=True)  83.6 us
    all_gather x1, waiting for transfers between devices, shards(): lax.all_gather(prompt_values, 'prompt', axis=1, tiled=True)  60.2 us
    all_gather x1, waiting for transfers between devices, shards(): lax.all_gather(prompt_keys, 'prompt', axis=1, tiled=True)  59.2 us
  transfers between devices with their start and end apart: 5, of which 5 were waited for; matrix products, arithmetic and copies ran while one was open for 3% of the time, Pallas kernels for 0%

commit v1 on v0

v1 whole, which is shorter than its diff:
```python
import functools
import math

import jax
import jax.numpy as jnp
from jax import lax
from jax.experimental import pallas as pl
from jax.experimental.pallas import tpu as pltpu
from jax.sharding import PartitionSpec as P

HD = 128
KVH = 4
GROUP = 4
HALF = 128
SCALE = 1.0 / math.sqrt(HD)
LOG2E = math.log2(math.e)
BF16 = jnp.bfloat16
F32 = jnp.float32


def nt_dot(a, b):
    return lax.dot_general(a, b, (((1,), (1,)), ((), ())), preferred_element_type=F32)


def nn_dot(a, b):
    return lax.dot_general(a, b, (((1,), (0,)), ((), ())), preferred_element_type=F32)


def pick_kernel(peers_ref, keys_ref, values_ref, out_ref):
    for p in range(out_ref.shape[0]):
        owner = peers_ref[p]
        both = jnp.concatenate(
            [keys_ref[owner].astype(F32), values_ref[owner].astype(F32)], axis=0
        )
        out_ref[p] = both.astype(BF16)


def pick(peers, keys, values):
    count, (_, rows, width) = peers.shape[0], keys.shape
    return pl.pallas_call(
        pick_kernel,
        out_shape=jax.ShapeDtypeStruct((count, 2 * rows, width), BF16),
        in_specs=[
            pl.BlockSpec(memory_space=pltpu.SMEM),
            pl.BlockSpec(memory_space=pltpu.VMEM),
            pl.BlockSpec(memory_space=pltpu.VMEM),
        ],
        out_specs=pl.BlockSpec(memory_space=pltpu.VMEM),
    )(peers, keys, values)


def attend_kernel(
    length_ref,
    query_ref,
    grad_ref,
    keys_ref,
    values_ref,
    front_ref,
    query_grad_ref,
    key_grad_ref,
    value_grad_ref,
    front_grad_ref,
):
    length = length_ref[0]
    rows = query_ref.shape[0]
    shards_n, both, _ = front_ref.shape
    own = both // 2
    front_len = shards_n * own
    front = front_ref[...].astype(F32)
    all_keys = jnp.concatenate(
        [front[:, :own].reshape(front_len, HD).astype(BF16), keys_ref[...]], axis=0
    )
    all_values = jnp.concatenate(
        [front[:, own:].reshape(front_len, HD).astype(BF16), values_ref[...]], axis=0
    )
    keys_across = jnp.transpose(all_keys)
    wide = GROUP * HALF
    key_ids = lax.broadcasted_iota(jnp.int32, (HALF, wide), 0)
    row_ids = lax.broadcasted_iota(jnp.int32, (HALF, wide), 1) % HALF
    allowed = key_ids <= row_ids
    live_ids = lax.broadcasted_iota(jnp.int32, (HALF, GROUP * HD), 0)
    key_total = None
    value_total = None
    for half in range(rows // HALF):
        span = slice(half * HALF, (half + 1) * HALF)
        reach = front_len + (half + 1) * HALF
        query = query_ref[span, :]
        grad = grad_ref[span, :]
        grad = jnp.where(live_ids + half * HALF < length, grad, jnp.zeros_like(grad))
        query = jnp.concatenate(
            [query[:, g * HD : (g + 1) * HD] for g in range(GROUP)], axis=0
        )
        grad = jnp.concatenate(
            [grad[:, g * HD : (g + 1) * HD] for g in range(GROUP)], axis=0
        )
        scores = nt_dot(all_keys[:reach], query)
        scores = jnp.concatenate(
            [
                scores[: reach - HALF],
                jnp.where(allowed, scores[reach - HALF :], -1e30),
            ],
            axis=0,
        )
        row_max = jnp.max(scores, axis=0, keepdims=True)
        weights = jnp.exp2((scores - row_max) * (SCALE * LOG2E))
        prob = weights * (1.0 / jnp.sum(weights, axis=0, keepdims=True))
        prob_low = prob.astype(BF16)
        dprob = nt_dot(all_values[:reach], grad)
        delta = jnp.sum(prob_low.astype(F32) * dprob, axis=0, keepdims=True)
        dscore = (prob * (dprob - delta)).astype(BF16)
        query_term = nn_dot(keys_across[:, :reach], dscore) * SCALE
        for g in range(GROUP):
            query_grad_ref[span, g * HD : (g + 1) * HD] = jnp.transpose(
                query_term[:, g * HALF : (g + 1) * HALF]
            ).astype(BF16)
        key_term = nn_dot(dscore, query) * SCALE
        value_term = nn_dot(prob_low, grad)
        if key_total is None:
            key_total, value_total = key_term, value_term
        else:
            done = key_total.shape[0]
            key_total = jnp.concatenate(
                [key_total + key_term[:done], key_term[done:]], axis=0
            )
            value_total = jnp.concatenate(
                [value_total + value_term[:done], value_term[done:]], axis=0
            )
    key_grad_ref[...] = key_total[front_len:].astype(BF16)
    value_grad_ref[...] = value_total[front_len:].astype(BF16)
    front_grad_ref[...] = jnp.concatenate(
        [
            key_total[:front_len].reshape(shards_n, own, HD),
            value_total[:front_len].reshape(shards_n, own, HD),
        ],
        axis=1,
    ).astype(BF16)


def attend(length, query, grad, keys, values, front):
    rows, query_width = query.shape
    key_width = keys.shape[1]
    shards_n, both, _ = front.shape
    wide = pl.BlockSpec((rows, GROUP * HD), lambda k: (0, k))
    narrow = pl.BlockSpec((rows, HD), lambda k: (0, k))
    front_spec = pl.BlockSpec((shards_n, both, HD), lambda k: (0, 0, k))
    return pl.pallas_call(
        attend_kernel,
        grid=(KVH,),
        out_shape=(
            jax.ShapeDtypeStruct((rows, query_width), BF16),
            jax.ShapeDtypeStruct((rows, key_width), BF16),
            jax.ShapeDtypeStruct((rows, key_width), BF16),
            jax.ShapeDtypeStruct(front.shape, BF16),
        ),
        in_specs=[
            pl.BlockSpec(memory_space=pltpu.SMEM),
            wide,
            wide,
            narrow,
            narrow,
            front_spec,
        ],
        out_specs=(wide, narrow, narrow, front_spec),
        compiler_params=pltpu.CompilerParams(vmem_limit_bytes=48 * 1024 * 1024),
    )(length, query, grad, keys, values, front)


def add_kernel(peers_ref, terms_ref, out_ref, total):
    total[...] = jnp.zeros_like(total)
    for p in range(terms_ref.shape[0]):
        owner = peers_ref[p]
        total[owner] = total[owner] + terms_ref[p].astype(F32)
    for owner in range(total.shape[0]):
        for k in range(KVH):
            out_ref[owner * KVH + k] = total[owner, :, k * HD : (k + 1) * HD].astype(BF16)


def add_by_prompt(peers, terms, num_prompts):
    _, both, width = terms.shape
    return pl.pallas_call(
        add_kernel,
        out_shape=jax.ShapeDtypeStruct((num_prompts * KVH, both, HD), BF16),
        in_specs=[
            pl.BlockSpec(memory_space=pltpu.SMEM),
            pl.BlockSpec(memory_space=pltpu.VMEM),
        ],
        out_specs=pl.BlockSpec(memory_space=pltpu.VMEM),
        scratch_shapes=[pltpu.VMEM((num_prompts, both, width), F32)],
    )(peers, terms)


def shards(query, resp_keys, resp_values, prompt_keys, prompt_values, out_grad, group, lengths):
    resp_count = lax.axis_size("resp")
    resp_index = lax.axis_index("resp")
    num_prompts, own, width = prompt_keys.shape
    peers = lax.dynamic_index_in_dim(
        group.reshape(-1, resp_count), resp_index, 1, keepdims=False
    )
    front = lax.all_to_all(pick(peers, prompt_keys, prompt_values), "prompt", 0, 0)
    query_grad, key_grad, value_grad, front_grad = attend(
        lengths, query[0], out_grad[0], resp_keys[0], resp_values[0], front
    )
    terms = lax.all_to_all(front_grad, "prompt", 0, 0)
    sums = add_by_prompt(peers, terms, num_prompts)
    parts = lax.all_to_all(sums, "resp", 0, 0)
    mine = jnp.sum(parts.astype(F32), 0).astype(BF16)
    spread = jnp.broadcast_to(mine[None], (resp_count,) + mine.shape)
    whole = lax.all_to_all(spread, "resp", 0, 0).astype(F32)
    whole = whole.reshape(num_prompts, KVH, 2, own, HD).transpose(2, 0, 3, 1, 4)
    whole = whole.reshape(2, num_prompts, own, width)
    return (query_grad[None], key_grad[None], value_grad[None], whole[0], whole[1])


def solution(mesh):
    return jax.shard_map(
        shards,
        mesh=mesh,
        in_specs=(
            P(("prompt", "resp"), None, None),
            P(("prompt", "resp"), None, None),
            P(("prompt", "resp"), None, None),
            P(None, "prompt", None),
            P(None, "prompt", None),
            P(("prompt", "resp"), None, None),
            P(),
            P(("prompt", "resp")),
        ),
        out_specs=(
            P(("prompt", "resp"), None, None),
            P(("prompt", "resp"), None, None),
            P(("prompt", "resp"), None, None),
            P(None, "prompt", None),
            P(None, "prompt", None),
        ),
        check_vma=False,
    )
```

time: 595 us -> 91.8 us (0.15)
  waiting for transfers between devices: 524 us -> 10.9 us
  blocking collectives: 0 us -> 49.8 us
  matrix products: 24.6 us -> 0 us
  between operations: 16.9 us -> 1.32 us
  other arithmetic: 13.7 us -> 0.06 us
  starting transfers between devices: 0.19 us -> 13.6 us
  Pallas kernels: 0 us -> 11.1 us
  local copies, waits for them, and re-layouts: 14.4 us -> 4.65 us
    psum x1 -> x0, waiting for transfers between devices: 223 us -> none  [shards(): lax.psum((local_keys, local_values), 'resp')]
    reduce_scatter x2 -> x0, waiting for transfers between devices: 180 us -> none  [the longest x1 96.4 us: shards(): lax.psum_scatter(spread_keys, 'prompt', scatter_dimension=1, tiled=True)]
    all_gather x2 -> x0, waiting for transfers between devices: 119 us -> none  [the longest x1 60.2 us: shards(): lax.all_gather(prompt_values, 'prompt', axis=1, tiled=True)]
    all_to_all x0 -> x3, blocking collectives: none -> 49.8 us  [the longest x1 21.7 us: shards(): parts = lax.all_to_all(sums, 'resp', 0, 0)]
    dot_general x20 -> x0, matrix products: 16.1 us -> none  [the longest x4 4.26 us: attend_backward(): jnp.einsum('gij,igd->jd', prob_low, head_grad, preferred_element_type=jnp...]
    all_to_all x0 -> x1, starting transfers between devices: none -> 13.6 us  [shards(): lax.all_to_all(pick(peers, prompt_keys, prompt_values), 'prompt', 0, 0)]
    pallas_call x0 -> x3, Pallas kernels: none -> 11.1 us  [the longest x1 7.79 us: attend(): pl.pallas_call(attend_kernel, grid=(KVH,), out_shape=(jax.ShapeDtypeStruc...]
    all_to_all x0 -> x1, waiting for transfers between devices: none -> 10.9 us  [shards(): lax.all_to_all(pick(peers, prompt_keys, prompt_values), 'prompt', 0, 0)]
  transfers between devices with their start and end apart: 5 -> 1, of which waited for: 5 -> 1; matrix products, arithmetic and copies ran while one was open for 3% -> 0% of each run, Pallas kernels for 0% -> 0%
where the time goes in v1:
time: 91.8 us; the launch traced here: 91.3 us
  blocking collectives  49.8 us (54%)
  starting transfers between devices  13.6 us (15%)
  Pallas kernels  11.1 us (12%)
  waiting for transfers between devices  10.9 us (12%)
  local copies, waits for them, and re-layouts  4.65 us (5%)
  between operations  1.32 us (1%)
    all_to_all x1, blocking collectives, shards(): parts = lax.all_to_all(sums, 'resp', 0, 0)  21.7 us
    all_to_all x1, blocking collectives, shards(): terms = lax.all_to_all(front_grad, 'prompt', 0, 0)  14.7 us
    all_to_all x1, starting transfers between devices, shards(): lax.all_to_all(pick(peers, prompt_keys, prompt_values), 'prompt', 0, 0)  13.6 us
    all_to_all x1, blocking collectives, shards(): whole = lax.all_to_all(spread, 'resp', 0, 0).astype(F32)  13.4 us
    all_to_all x1, waiting for transfers between devices, shards(): lax.all_to_all(pick(peers, prompt_keys, prompt_values), 'prompt', 0, 0)  10.9 us
    pallas_call x1, Pallas kernels, attend(): pl.pallas_call(attend_kernel, grid=(KVH,), out_shape=(jax.ShapeDtypeStruc...  7.79 us
    unnamed x10, local copies, waits for them, and re-layouts  3.13 us
  transfers between devices with their start and end apart: 1, of which 1 were waited for; matrix products, arithmetic and copies ran while one was open for 0% of the time, Pallas kernels for 0%

profile of v1, /device:TPU:1, one launch (start us, length us, event | category | flops | bytes accessed | tf_op | source)
XLA Modules:
  0.0 91.3 jit_solution(12208782577571967710)
XLA Ops:
  0.6 0.0 copy-start.4
  0.6 0.7 copy-done.4
  1.3 0.1 reshape.23
  1.4 0.7 dynamic-slice_reduce_fusion.peers_ref
  2.1 1.6 %shard_map.119 = bf16[16,16,512]{2,1,0:T(8,128)(2,1)} custom-call(s32[16]{0:T(128)} %dynamic-slice_reduce_fusion.peers_ref, bf16[8,8,512]{2,1,0:T(8,128)(2,1)} %keys_ref.1, bf16[8,8,512]{2,1,0:T(8,128)(2,1)} %values_ref.1), custom_call_target="tpu_custom_call" | custom-call | tf_op jit(solution)/shard_map/pallas_call | solution.py:40
  3.7 0.0 copy-start.2
  3.7 0.0 copy-start.3
  3.7 13.6 %all-to-all-start = ((bf16[16,16,512]{2,1,0:T(8,128)(2,1)}), bf16[16,16,512]{2,1,0:T(8,128)(2,1)S(1)}, u32[]{:S(2)}, u32[]{:S(2)}) async-start(bf16[16,16,512]{2,1,0:T(8,128)(2,1)} %shard_map.119), calls=%async_computation | async-start | bytes 524288 | tf_op jit(solution)/shard_map/all_to_all | solution.py:199
  17.9 10.9 %all-to-all-done.front_ref = bf16[16,16,512]{2,1,0:T(8,128)(2,1)S(1)} async-done(((bf16[16,16,512]{2,1,0:T(8,128)(2,1)}), bf16[16,16,512]{2,1,0:T(8,128)(2,1)S(1)}, u32[]{:S(2)}, u32[]{:S(2)}) %all-to-all-start) | async-done | bytes 262176 | tf_op jit(solution)/shard_map/all_to_all | solution.py:199
  28.8 0.0 copy-done.2
  28.8 0.0 copy-done.3
  28.8 0.0 copy-start
  28.8 1.2 %copy-done = bf16[1,256,2048]{2,1,0:T(8,128)(2,1)S(1)} copy-done((bf16[1,256,2048]{2,1,0:T(8,128)(2,1)S(1)}, bf16[1,256,2048]{2,1,0:T(8,128)(2,1)}, u32[]{:S(2)}) %copy-start) | copy-done | bytes 1048600
  30.0 0.0 copy-start.1
  30.0 1.2 %copy-done.1 = bf16[1,256,2048]{2,1,0:T(8,128)(2,1)S(1)} copy-done((bf16[1,256,2048]{2,1,0:T(8,128)(2,1)S(1)}, bf16[1,256,2048]{2,1,0:T(8,128)(2,1)}, u32[]{:S(2)}) %copy-start.1) | copy-done | bytes 1048600
  31.2 7.8 %shard_map.120 = (bf16[256,2048]{1,0:T(8,128)(2,1)}, bf16[256,512]{1,0:T(8,128)(2,1)}, bf16[256,512]{1,0:T(8,128)(2,1)}, bf16[16,16,512]{2,1,0:T(8,128)(2,1)S(1)}) custom-call(s32[1]{0:T(128)S(6)} %copy.13.length_ref, bf16[256,2048]{1,0:T(8,128)(2,1)S(1)} %bitcast.15, bf16[256,2048]{1,0:T(8,128)(2,1)S(1)} %bitcast.16, bf16[256,512]{1,0:T(8,128)(2,1)S(1)} %bitcast.17, ...), custom_call_target="tpu_custom_call" | custom-call | tf_op jit(solution)/shard_map/pallas_call | solution.py:146
  39.0 14.7 %all_to_all.20.terms_ref = bf16[16,16,512]{2,1,0:T(8,128)(2,1)} all-to-all(bf16[16,16,512]{2,1,0:T(8,128)(2,1)S(1)} %get-tuple-element.12), channel_id=1, replica_groups=mesh['prompt'=16,'resp'=32] {'prompt'}, dimensions={0} | all-to-all | bytes 524288 | tf_op jit(solution)/shard_map/all_to_all | solution.py:203
  53.7 1.7 %shard_map.121 = bf16[32,16,128]{2,1,0:T(8,128)(2,1)} custom-call(s32[16]{0:T(128)} %dynamic-slice_reduce_fusion.peers_ref, bf16[16,16,512]{2,1,0:T(8,128)(2,1)} %all_to_all.20.terms_ref), custom_call_target="tpu_custom_call" | custom-call | tf_op jit(solution)/shard_map/pallas_call | solution.py:180
  55.4 21.7 %all_to_all.21 = bf16[32,16,128]{2,1,0:T(8,128)(2,1)S(1)} all-to-all(bf16[32,16,128]{2,1,0:T(8,128)(2,1)} %shard_map.121), channel_id=1, replica_groups=mesh['prompt'=16,'resp'=32] {'resp'}, dimensions={0} | all-to-all | bytes 262144 | tf_op jit(solution)/shard_map/all_to_all | solution.py:205
  77.2 13.4 %all_to_all.22 = bf16[32,16,128]{2,1,0:T(8,128)(2,1)S(1)} all-to-all(bf16[32,16,128]{2,1,0:T(8,128)(2,1)S(1)} %broadcast_in_dim.18), channel_id=1, replica_groups=mesh['prompt'=16,'resp'=32] {'resp'}, dimensions={0} | all-to-all | bytes 262144 | tf_op jit(solution)/shard_map/all_to_all | solution.py:208
  90.6 0.7 slice_bitcast_fusion
  (3 shorter events, 0.1 us)
Async XLA Ops:
  0.6 0.7 copy-start.4
  3.7 25.1 %copy-start.2 = (bf16[1,256,512]{2,1,0:T(8,128)(2,1)S(1)}, bf16[1,256,512]{2,1,0:T(8,128)(2,1)}, u32[]{:S(2)}) copy-start(bf16[1,256,512]{2,1,0:T(8,128)(2,1)} %param.9) | copy-start | bytes 786436
  3.7 25.1 %copy-start.3 = (bf16[1,256,512]{2,1,0:T(8,128)(2,1)S(1)}, bf16[1,256,512]{2,1,0:T(8,128)(2,1)}, u32[]{:S(2)}) copy-start(bf16[1,256,512]{2,1,0:T(8,128)(2,1)} %param.10) | copy-start | bytes 786436
  3.7 25.1 %all-to-all-start = ((bf16[16,16,512]{2,1,0:T(8,128)(2,1)}), bf16[16,16,512]{2,1,0:T(8,128)(2,1)S(1)}, u32[]{:S(2)}, u32[]{:S(2)}) async-start(bf16[16,16,512]{2,1,0:T(8,128)(2,1)} %shard_map.119), calls=%async_computation | async-start | bytes 524288 | tf_op jit(solution)/shard_map/all_to_all | solution.py:199
  28.8 1.2 %copy-start = (bf16[1,256,2048]{2,1,0:T(8,128)(2,1)S(1)}, bf16[1,256,2048]{2,1,0:T(8,128)(2,1)}, u32[]{:S(2)}) copy-start(bf16[1,256,2048]{2,1,0:T(8,128)(2,1)} %param.8) | copy-start | bytes 3145732
  30.0 1.2 %copy-start.1 = (bf16[1,256,2048]{2,1,0:T(8,128)(2,1)S(1)}, bf16[1,256,2048]{2,1,0:T(8,128)(2,1)}, u32[]{:S(2)}) copy-start(bf16[1,256,2048]{2,1,0:T(8,128)(2,1)} %param.13) | copy-start | bytes 3145732

commit v2 on v1

v2 whole, which is shorter than its diff:
```python
import functools
import math

import jax
import jax.numpy as jnp
from jax import lax
from jax.experimental import pallas as pl
from jax.experimental.pallas import tpu as pltpu
from jax.sharding import Mesh
from jax.sharding import PartitionSpec as P

HD = 128
KVH = 4
GROUP = 4
CORES = 2
HALF = 128
SCALE = 1.0 / math.sqrt(HD)
LOG2E = math.log2(math.e)
BF16 = jnp.bfloat16
F32 = jnp.float32
SMEM = pl.BlockSpec(memory_space=pltpu.SMEM)
VMEM = pl.BlockSpec(memory_space=pltpu.VMEM)


def nt_dot(a, b):
    return lax.dot_general(a, b, (((1,), (1,)), ((), ())), preferred_element_type=F32)


def nn_dot(a, b):
    return lax.dot_general(a, b, (((1,), (0,)), ((), ())), preferred_element_type=F32)


def exp_scaled(x):
    return jnp.exp2(x * (SCALE * LOG2E))


def stack_heads(block, half, k=0):
    span = slice(half * HALF, (half + 1) * HALF)
    return jnp.concatenate(
        [block[span, h * HD : (h + 1) * HD] for h in range(k * GROUP, (k + 1) * GROUP)],
        axis=0,
    )


def live_grad(grad_ref, length, half, k=0):
    grad = stack_heads(grad_ref, half, k)
    row_ids = lax.broadcasted_iota(jnp.int32, grad.shape, 0) % HALF
    return jnp.where(row_ids + half * HALF < length, grad, jnp.zeros_like(grad))


def causal(scores):
    reach, wide = scores.shape
    key_ids = lax.broadcasted_iota(jnp.int32, (HALF, wide), 0)
    row_ids = lax.broadcasted_iota(jnp.int32, (HALF, wide), 1) % HALF
    last = jnp.where(key_ids <= row_ids, scores[reach - HALF :], -1e30)
    if reach == HALF:
        return last
    return jnp.concatenate([scores[: reach - HALF], last], axis=0)


def front_parts(front_ref, k=0):
    shards_n, both, _ = front_ref.shape
    front = front_ref[:, :, k * HD : (k + 1) * HD].astype(F32)
    keys, values = front[:, : both // 2], front[:, both // 2 :]
    return (
        keys.reshape(shards_n * both // 2, HD).astype(BF16),
        values.reshape(shards_n * both // 2, HD).astype(BF16),
    )


def pick_kernel(group_ref, keys_ref, values_ref, out_ref):
    place_along = lax.axis_index("chip") * CORES + lax.axis_index("core")
    count = out_ref.shape[0]
    stride = group_ref.shape[0] // count
    for p in range(count):
        owner = group_ref[p * stride + place_along]
        both = jnp.concatenate(
            [keys_ref[owner].astype(F32), values_ref[owner].astype(F32)], axis=0
        )
        out_ref[p] = both.astype(BF16)


def pick(group, keys, values, count):
    _, rows, width = keys.shape
    return pl.pallas_call(
        pick_kernel,
        out_shape=jax.ShapeDtypeStruct((count, 2 * rows, width), BF16),
        in_specs=[SMEM, VMEM, VMEM],
        out_specs=VMEM,
        compiler_params=params(56),
    )(group, keys, values)


def own_kernel(length_ref, query_ref, grad_ref, keys_ref, values_ref, stats_ref):
    length = length_ref[0]
    for k in range(KVH):
        features = slice(k * HD, (k + 1) * HD)
        for half in range(query_ref.shape[0] // HALF):
            reach = (half + 1) * HALF
            query = stack_heads(query_ref, half, k)
            grad = live_grad(grad_ref, length, half, k)
            scores = causal(nt_dot(keys_ref[:reach, features], query))
            top = jnp.max(scores, axis=0, keepdims=True)
            weights = exp_scaled(scores - top)
            dprob = nt_dot(values_ref[:reach, features], grad)
            total = jnp.sum(weights, axis=0, keepdims=True)
            dot = jnp.sum(weights * dprob, axis=0, keepdims=True)
            fill = jnp.zeros((5, top.shape[1]), F32)
            stats_ref[k, half] = jnp.concatenate([top, total, dot, fill], axis=0)


def front_kernel(
    length_ref, query_ref, grad_ref, front_ref, stats_ref, front_grad_ref, full_ref
):
    length = length_ref[0]
    shards_n, _, both, _ = front_grad_ref.shape
    for k in range(KVH):
        keys, values = front_parts(front_ref, k)
        key_total, value_total = 0.0, 0.0
        for half in range(query_ref.shape[0] // HALF):
            query = stack_heads(query_ref, half, k)
            grad = live_grad(grad_ref, length, half, k)
            stats = stats_ref[k, half]
            own_top, own_total, own_dot = stats[0:1], stats[1:2], stats[2:3]
            scores = nt_dot(keys, query)
            top = jnp.maximum(jnp.max(scores, axis=0, keepdims=True), own_top)
            weights = exp_scaled(scores - top)
            rescale = exp_scaled(own_top - top)
            total = jnp.sum(weights, axis=0, keepdims=True) + own_total * rescale
            inverse = 1.0 / total
            prob = weights * inverse
            prob_low = prob.astype(BF16)
            dprob = nt_dot(values, grad)
            delta = jnp.sum(prob * dprob, axis=0, keepdims=True) + own_dot * (
                rescale * inverse
            )
            dscore = (prob * (dprob - delta)).astype(BF16)
            key_total = key_total + nn_dot(dscore, query)
            value_total = value_total + nn_dot(prob_low, grad)
            fill = jnp.zeros((5, top.shape[1]), F32)
            full_ref[k, half] = jnp.concatenate([top, inverse, delta, fill], axis=0)
        front_grad_ref[:, k] = jnp.concatenate(
            [
                (key_total * SCALE).reshape(shards_n, both // 2, HD),
                value_total.reshape(shards_n, both // 2, HD),
            ],
            axis=1,
        ).astype(BF16)


def rest_kernel(
    length_ref,
    query_ref,
    grad_ref,
    keys_ref,
    values_ref,
    front_ref,
    full_ref,
    query_grad_ref,
    key_grad_ref,
    value_grad_ref,
):
    length = length_ref[0]
    front_keys, front_values = front_parts(front_ref)
    front_len = front_keys.shape[0]
    all_keys = jnp.concatenate([front_keys, keys_ref[...]], axis=0)
    all_values = jnp.concatenate([front_values, values_ref[...]], axis=0)
    keys_across = jnp.transpose(all_keys)
    key_total, value_total = None, None
    for half in range(query_ref.shape[0] // HALF):
        reach = front_len + (half + 1) * HALF
        span = slice(half * HALF, (half + 1) * HALF)
        query = stack_heads(query_ref, half)
        grad = live_grad(grad_ref, length, half)
        full = full_ref[half]
        top, inverse, delta = full[0:1], full[1:2], full[2:3]
        scores = causal(nt_dot(all_keys[:reach], query))
        prob = exp_scaled(scores - top) * inverse
        dprob = nt_dot(all_values[:reach], grad)
        dscore = (prob * (dprob - delta)).astype(BF16)
        query_term = nn_dot(keys_across[:, :reach], dscore) * SCALE
        for g in range(GROUP):
            query_grad_ref[span, g * HD : (g + 1) * HD] = jnp.transpose(
                query_term[:, g * HALF : (g + 1) * HALF]
            ).astype(BF16)
        key_term = nn_dot(dscore[front_len:], query)
        value_term = nn_dot(prob[front_len:].astype(BF16), grad)
        if key_total is None:
            key_total, value_total = key_term, value_term
        else:
            done = key_total.shape[0]
            key_total = jnp.concatenate(
                [key_total + key_term[:done], key_term[done:]], axis=0
            )
            value_total = jnp.concatenate(
                [value_total + value_term[:done], value_term[done:]], axis=0
            )
    key_grad_ref[...] = (key_total * SCALE).astype(BF16)
    value_grad_ref[...] = value_total.astype(BF16)


def attention_specs(rows, shards_n, both):
    wide = pl.BlockSpec((rows, GROUP * HD), lambda k: (0, k))
    narrow = pl.BlockSpec((rows, HD), lambda k: (0, k))
    front = pl.BlockSpec((shards_n, both, HD), lambda k: (0, 0, k))
    stats = pl.BlockSpec(
        (None, rows // HALF, 8, GROUP * HALF), lambda k: (k, 0, 0, 0)
    )
    return wide, narrow, front, stats


def params(mib):
    return pltpu.CompilerParams(vmem_limit_bytes=mib * 1024 * 1024)


def cost(matmuls, keys):
    flops = 2 * KVH * GROUP * 256 * keys * HD * matmuls
    return pl.CostEstimate(
        flops=flops, bytes_accessed=3 << 20, transcendentals=KVH * GROUP * 256 * keys
    )


def own_stats(length, query, grad, keys, values):
    rows = query.shape[0]
    return pl.pallas_call(
        own_kernel,
        out_shape=jax.ShapeDtypeStruct((KVH, rows // HALF, 8, GROUP * HALF), F32),
        in_specs=[SMEM, VMEM, VMEM, VMEM, VMEM],
        out_specs=VMEM,
        compiler_params=params(16),
        cost_estimate=cost(2, 256),
    )(length, query, grad, keys, values)


def front_part(length, query, grad, front, own):
    shards_n, both, _ = front.shape
    return pl.pallas_call(
        front_kernel,
        out_shape=(
            jax.ShapeDtypeStruct((shards_n, KVH, both, HD), BF16),
            jax.ShapeDtypeStruct(own.shape, F32),
        ),
        in_specs=[SMEM, VMEM, VMEM, VMEM, VMEM],
        out_specs=(VMEM, VMEM),
        compiler_params=params(16),
        cost_estimate=cost(4, 128),
    )(length, query, grad, front, own)


def rest_part(length, query, grad, keys, values, front, full):
    shards_n, both, _ = front.shape
    wide, narrow, front_spec, stats = attention_specs(query.shape[0], shards_n, both)
    return pl.pallas_call(
        rest_kernel,
        grid=(KVH,),
        out_shape=(
            jax.ShapeDtypeStruct(query.shape, BF16),
            jax.ShapeDtypeStruct(keys.shape, BF16),
            jax.ShapeDtypeStruct(values.shape, BF16),
        ),
        in_specs=[SMEM, wide, wide, narrow, narrow, front_spec, stats],
        out_specs=(wide, narrow, narrow),
        compiler_params=params(24),
        cost_estimate=cost(5, 384),
    )(length, query, grad, keys, values, front, full)


def add_kernel(num_prompts, owners_ref, terms_ref, _, out_ref):
    count = terms_ref.shape[0]
    total = out_ref.shape[1]
    rows = total // num_prompts
    row_ids = lax.broadcasted_iota(jnp.int32, (total, count), 0)
    col_ids = lax.broadcasted_iota(jnp.int32, (total, count), 1)
    hit = (owners_ref[...] == row_ids // rows) & (row_ids % rows == col_ids % rows)
    sums = nn_dot(jnp.where(hit, 1.0, 0.0).astype(BF16), terms_ref[...]).astype(BF16)
    out_ref[...] = jnp.broadcast_to(sums[None], out_ref.shape)


def add_by_prompt(owners, terms, after, num_prompts, rows, copies):
    return pl.pallas_call(
        functools.partial(add_kernel, num_prompts),
        out_shape=jax.ShapeDtypeStruct((copies, rows * num_prompts, HD), BF16),
        in_specs=[VMEM, VMEM, pl.BlockSpec(memory_space=pl.ANY)],
        out_specs=VMEM,
        compiler_params=params(4),
    )(owners, terms, after)


def place_kernel(parts_ref, key_ref, value_ref):
    prompts, own, _ = key_ref.shape
    blocks = parts_ref.shape[0] // (2 * KVH)
    rows = own // blocks
    size = prompts * own
    to = lax.broadcasted_iota(jnp.int32, (size, size), 0)
    at = lax.broadcasted_iota(jnp.int32, (size, size), 1)
    prompt, row = to // own, to % own
    hit = at == (row // rows) * (rows * prompts) + prompt * rows + row % rows
    move = jnp.where(hit, 1.0, 0.0).astype(BF16)
    for k in range(KVH):
        for side, out_ref in enumerate((key_ref, value_ref)):
            first = (k * 2 + side) * blocks
            block = parts_ref[first : first + blocks].reshape(size, HD)
            out_ref[:, :, k * HD : (k + 1) * HD] = nn_dot(move, block).reshape(
                prompts, own, HD
            )


def place(parts, shape):
    return pl.pallas_call(
        place_kernel,
        out_shape=(jax.ShapeDtypeStruct(shape, F32), jax.ShapeDtypeStruct(shape, F32)),
        in_specs=[VMEM],
        out_specs=(VMEM, VMEM),
        compiler_params=params(4),
    )(parts)


def shards(query, resp_keys, resp_values, prompt_keys, prompt_values, out_grad, group, lengths):
    places, chips = lax.axis_size("prompt"), lax.axis_size("chip")
    num_prompts, own, width = prompt_keys.shape
    wanted = pick(group, prompt_keys, prompt_values, places)
    front = lax.all_to_all(wanted, "prompt", 0, 0)
    query, grad, keys, values = query[0], out_grad[0], resp_keys[0], resp_values[0]
    stats = own_stats(lengths, query, grad, keys, values)
    front_grad, full = front_part(lengths, query, grad, front, stats)
    rows = 2 * own * width // (chips * HD)
    terms = lax.all_to_all(
        front_grad.reshape(places * chips, rows, HD), ("prompt", "chip"), 0, 0
    )
    query_grad, key_grad, value_grad = rest_part(
        lengths, query, grad, keys, values, front, full
    )
    terms = lax.all_gather(terms, "core", axis=0).reshape(-1, HD)
    owners = jnp.repeat(jnp.transpose(group.reshape(-1, CORES)).reshape(-1), rows)
    sums = add_by_prompt(owners[None], terms, key_grad, num_prompts, rows, chips)
    parts = lax.all_to_all(sums, "chip", 0, 0)
    prompt_key_grad, prompt_value_grad = place(parts, prompt_keys.shape)
    return (
        query_grad[None],
        key_grad[None],
        value_grad[None],
        prompt_key_grad,
        prompt_value_grad,
    )


def solution(mesh):
    places, resps = mesh.devices.shape
    mesh = Mesh(
        mesh.devices.reshape(places, resps // CORES, CORES), ("prompt", "chip", "core")
    )
    every = ("prompt", "chip", "core")
    row = P(every, None, None)
    front = P(None, "prompt", None)
    return jax.shard_map(
        shards,
        mesh=mesh,
        in_specs=(row, row, row, front, front, row, P(), P(every)),
        out_specs=(row, row, row, front, front),
        check_vma=False,
    )
```

time: 91.8 us -> 75.7 us (0.82)
  blocking collectives: 49.8 us -> 14.9 us
  starting transfers between devices: 13.6 us -> 28.7 us
  waiting for transfers between devices: 10.9 us -> 14.1 us
  Pallas kernels: 11.1 us -> 12.8 us
  local copies, waits for them, and re-layouts: 4.65 us -> 3 us
    all_to_all x3 -> x1, blocking collectives: 49.8 us -> 10.7 us  [shards(): parts = lax.all_to_all(sums, 'chip', 0, 0)]
    all_to_all x1 -> x2, starting transfers between devices: 13.6 us -> 28.7 us  [the longest x1 15.2 us: shards(): lax.all_to_all(front_grad.reshape(places * chips, rows, HD), ('prompt', '...]
    all_gather x0 -> x1, blocking collectives: none -> 4.18 us  [shards(): terms = lax.all_gather(terms, 'core', axis=0).reshape(-1, HD)]
    all_to_all x1 -> x2, waiting for transfers between devices: 10.9 us -> 14.1 us  [the longest x1 7.32 us: shards(): lax.all_to_all(front_grad.reshape(places * chips, rows, HD), ('prompt', '...]
    pallas_call x2 -> x5, Pallas kernels: 9.51 us -> 11.2 us  [the longest x1 5.54 us: rest_part(): pl.pallas_call(rest_kernel, grid=(KVH,), out_shape=(jax.ShapeDtypeStruct(...]
    unnamed x10 -> x17, local copies, waits for them, and re-layouts: 3.13 us -> 2.47 us
  transfers between devices with their start and end apart: 1 -> 2, of which waited for: 1 -> 2; matrix products, arithmetic and copies ran while one was open for 0% -> 1% of each run, Pallas kernels for 0% -> 9%
where the time goes in v2:
time: 75.7 us; the launch traced here: 74.9 us
  starting transfers between devices  28.7 us (38%)
  blocking collectives  14.9 us (20%)
  waiting for transfers between devices  14.1 us (19%)
  Pallas kernels  12.8 us (17%)
  local copies, waits for them, and re-layouts  3 us (4%)
  between operations  1.38 us (2%)
    all_to_all x1, starting transfers between devices, shards(): lax.all_to_all(front_grad.reshape(places * chips, rows, HD), ('prompt', '...  15.2 us
    all_to_all x1, starting transfers between devices, shards(): front = lax.all_to_all(wanted, 'prompt', 0, 0)  13.6 us
    all_to_all x1, blocking collectives, shards(): parts = lax.all_to_all(sums, 'chip', 0, 0)  10.7 us
    all_to_all x1, waiting for transfers between devices, shards(): lax.all_to_all(front_grad.reshape(places * chips, rows, HD), ('prompt', '...  7.32 us
    all_to_all x1, waiting for transfers between devices, shards(): front = lax.all_to_all(wanted, 'prompt', 0, 0)  6.83 us
    pallas_call x1, Pallas kernels, rest_part(): pl.pallas_call(rest_kernel, grid=(KVH,), out_shape=(jax.ShapeDtypeStruct(...  5.54 us
    all_gather x1, blocking collectives, shards(): terms = lax.all_gather(terms, 'core', axis=0).reshape(-1, HD)  4.18 us
    pallas_call x1, Pallas kernels, front_part(): pl.pallas_call(front_kernel, out_shape=(jax.ShapeDtypeStruct((shards_n, K...  2.99 us
  transfers between devices with their start and end apart: 2, of which 2 were waited for; matrix products, arithmetic and copies ran while one was open for 1% of the time, Pallas kernels for 9%

profile of v2, /device:TPU:1, one launch (start us, length us, event | category | flops | bytes accessed | tf_op | source)
XLA Modules:
  0.0 74.9 jit_solution(12343398891349248887)
XLA Ops:
  0.6 1.6 %shard_map.119 = bf16[16,16,512]{2,1,0:T(8,128)(2,1)} custom-call(s32[512]{0:T(512)} %group_ref.1, bf16[8,8,512]{2,1,0:T(8,128)(2,1)} %keys_ref.1, bf16[8,8,512]{2,1,0:T(8,128)(2,1)} %values_ref.1), custom_call_target="tpu_custom_call" | custom-call | tf_op jit(solution)/shard_map/pallas_call | solution.py:85
  2.3 0.0 copy-start.4
  2.3 0.0 copy-start.5
  2.3 13.6 %all-to-all-start = ((bf16[16,16,512]{2,1,0:T(8,128)(2,1)}), bf16[16,16,512]{2,1,0:T(8,128)(2,1)S(1)}, u32[]{:S(2)}, u32[]{:S(2)}) async-start(bf16[16,16,512]{2,1,0:T(8,128)(2,1)} %shard_map.119), calls=%async_computation | async-start | bytes 524288 | tf_op jit(solution)/shard_map/all_to_all | solution.py:322
  16.5 0.0 copy-done.4
  16.5 0.0 copy-done.5
  16.5 0.0 copy-start
  16.5 1.2 %copy-done = bf16[1,256,2048]{2,1,0:T(8,128)(2,1)S(1)} copy-done((bf16[1,256,2048]{2,1,0:T(8,128)(2,1)S(1)}, bf16[1,256,2048]{2,1,0:T(8,128)(2,1)}, u32[]{:S(2)}) %copy-start) | copy-done | bytes 1048600
  17.7 0.0 copy-start.2
  17.7 1.2 %copy-done.2 = bf16[1,256,2048]{2,1,0:T(8,128)(2,1)S(1)} copy-done((bf16[1,256,2048]{2,1,0:T(8,128)(2,1)S(1)}, bf16[1,256,2048]{2,1,0:T(8,128)(2,1)}, u32[]{:S(2)}) %copy-start.2) | copy-done | bytes 1048600
  18.9 0.0 copy-start.1
  18.9 0.0 copy-start.3
  18.9 1.5 %shard_map.120.stats_ref = f32[4,2,8,512]{3,2,1,0:T(8,128)S(1)} custom-call(s32[1]{0:T(128)S(6)} %copy.16.length_ref, bf16[256,2048]{1,0:T(8,128)(2,1)S(1)} %bitcast.12, bf16[256,2048]{1,0:T(8,128)(2,1)S(1)} %bitcast.15, bf16[256,512]{1,0:T(8,128)(2,1)S(1)} %bitcast.19, bf16[256,512]{1,0:T(8,128)(2,1)S(1)} %bitcast.21), custom_call_target="tpu_custom_call" | custom-call | flops 536870912 | bytes 3145728 | tf_op jit(solution)/shard_map/pallas_call | solution.py:225
  20.5 6.8 %all-to-all-done.front_ref = bf16[16,16,512]{2,1,0:T(8,128)(2,1)S(1)} async-done(((bf16[16,16,512]{2,1,0:T(8,128)(2,1)}), bf16[16,16,512]{2,1,0:T(8,128)(2,1)S(1)}, u32[]{:S(2)}, u32[]{:S(2)}) %all-to-all-start) | async-done | bytes 262176 | tf_op jit(solution)/shard_map/all_to_all | solution.py:322
  27.3 0.0 copy-done.1
  27.3 0.0 copy-done.3
  27.3 3.0 %shard_map.121 = (bf16[16,4,16,128]{3,2,1,0:T(8,128)(2,1)}, f32[4,2,8,512]{3,2,1,0:T(8,128)S(1)}) custom-call(s32[1]{0:T(128)S(6)} %copy.16.length_ref, bf16[256,2048]{1,0:T(8,128)(2,1)S(1)} %bitcast.13, bf16[256,2048]{1,0:T(8,128)(2,1)S(1)} %bitcast.16, bf16[16,16,512]{2,1,0:T(8,128)(2,1)S(1)} %all-to-all-done.front_ref, ...), custom_call_target="tpu_custom_call" | custom-call | flops 536870912 | bytes 3145728 | tf_op jit(solution)/shard_map/pallas_call | solution.py:237
  30.3 0.0 copy-start.7
  30.3 15.2 %all-to-all-start.1 = ((bf16[256,4,128]{2,1,0:T(4,128)(2,1)}), bf16[256,4,128]{2,1,0:T(4,128)(2,1)S(1)}, u32[]{:S(2)}, u32[]{:S(2)}) async-start(bf16[256,4,128]{2,1,0:T(4,128)(2,1)} %bitcast.8), calls=%async_computation.1 | async-start | bytes 524288 | tf_op jit(solution)/shard_map/all_to_all | solution.py:327
  45.5 0.0 copy-done.7
  45.5 0.1 reshape.22
  45.7 0.1 copy.14
  45.7 0.1 broadcast_in_dim.15
  45.9 0.2 broadcast_in_dim_reshape.3.owners_ref
  46.1 5.5 %shard_map.122 = (bf16[256,2048]{1,0:T(8,128)(2,1)}, bf16[256,512]{1,0:T(8,128)(2,1)}, bf16[256,512]{1,0:T(8,128)(2,1)}) custom-call(s32[1]{0:T(128)S(6)} %copy.16.length_ref, bf16[256,2048]{1,0:T(8,128)(2,1)S(1)} %bitcast.14, bf16[256,2048]{1,0:T(8,128)(2,1)S(1)} %bitcast.17, bf16[256,512]{1,0:T(8,128)(2,1)S(1)} %bitcast.20, bf16[256,512]{1,0:T(8,128)(2,1)S(1)} %bitcast.22, ...), custom_call_target="tpu_custom_call" | custom-call | flops 2013265920 | bytes 3145728 | tf_op jit(solution)/shard_map/pallas_call | solution.py:253
  51.6 0.0 copy-start.6
  51.6 7.3 %all-to-all-done.1 = bf16[256,4,128]{2,1,0:T(4,128)(2,1)S(1)} async-done(((bf16[256,4,128]{2,1,0:T(4,128)(2,1)}), bf16[256,4,128]{2,1,0:T(4,128)(2,1)S(1)}, u32[]{:S(2)}, u32[]{:S(2)}) %all-to-all-start.1) | async-done | bytes 262176 | tf_op jit(solution)/shard_map/all_to_all | solution.py:327
  58.9 4.2 %all-gather = bf16[512,4,128]{2,1,0:T(4,128)(2,1)S(1)} all-gather(bf16[256,4,128]{2,1,0:T(4,128)(2,1)S(1)} %all-to-all-done.1), channel_id=2, replica_groups=mesh['prompt'=16,'chip'=16,'core'=2] {'core'}, dimensions={0}, use_global_device_ids=true | all-gather | bytes 786432 | tf_op jit(solution)/shard_map/all_gather | solution.py:333
  63.1 0.0 copy-done.6
  63.1 0.2 shard_map.123
  63.3 10.7 %all_to_all.15.parts_ref = bf16[16,32,128]{2,1,0:T(8,128)(2,1)S(1)} all-to-all(bf16[16,32,128]{2,1,0:T(8,128)(2,1)S(1)} %shard_map.123), channel_id=1, replica_groups=mesh['prompt'=16,'chip'=16,'core'=2] {'chip'}, dimensions={0} | all-to-all | bytes 262144 | tf_op jit(solution)/shard_map/all_to_all | solution.py:336
  74.0 0.9 %shard_map.124 = (f32[8,8,512]{2,1,0:T(8,128)}, f32[8,8,512]{2,1,0:T(8,128)}) custom-call(bf16[16,32,128]{2,1,0:T(8,128)(2,1)S(1)} %all_to_all.15.parts_ref), custom_call_target="tpu_custom_call" | custom-call | tf_op jit(solution)/shard_map/pallas_call | solution.py:309
  (1 shorter events, 0.0 us)
Async XLA Ops:
  2.3 14.2 %copy-start.4 = (bf16[1,256,512]{2,1,0:T(8,128)(2,1)S(1)}, bf16[1,256,512]{2,1,0:T(8,128)(2,1)}, u32[]{:S(2)}) copy-start(bf16[1,256,512]{2,1,0:T(8,128)(2,1)} %param.9) | copy-start | bytes 786436
  2.3 14.2 %copy-start.5 = (bf16[1,256,512]{2,1,0:T(8,128)(2,1)S(1)}, bf16[1,256,512]{2,1,0:T(8,128)(2,1)}, u32[]{:S(2)}) copy-start(bf16[1,256,512]{2,1,0:T(8,128)(2,1)} %param.10) | copy-start | bytes 786436
  2.3 25.1 %all-to-all-start = ((bf16[16,16,512]{2,1,0:T(8,128)(2,1)}), bf16[16,16,512]{2,1,0:T(8,128)(2,1)S(1)}, u32[]{:S(2)}, u32[]{:S(2)}) async-start(bf16[16,16,512]{2,1,0:T(8,128)(2,1)} %shard_map.119), calls=%async_computation | async-start | bytes 524288 | tf_op jit(solution)/shard_map/all_to_all | solution.py:322
  16.5 1.2 %copy-start = (bf16[1,256,2048]{2,1,0:T(8,128)(2,1)S(1)}, bf16[1,256,2048]{2,1,0:T(8,128)(2,1)}, u32[]{:S(2)}) copy-start(bf16[1,256,2048]{2,1,0:T(8,128)(2,1)} %param.8) | copy-start | bytes 3145732
  17.7 1.2 %copy-start.2 = (bf16[1,256,2048]{2,1,0:T(8,128)(2,1)S(1)}, bf16[1,256,2048]{2,1,0:T(8,128)(2,1)}, u32[]{:S(2)}) copy-start(bf16[1,256,2048]{2,1,0:T(8,128)(2,1)} %param.13) | copy-start | bytes 3145732
  18.9 8.4 %copy-start.1 = (bf16[1,256,2048]{2,1,0:T(8,128)(2,1)S(1)}, bf16[1,256,2048]{2,1,0:T(8,128)(2,1)}, u32[]{:S(2)}) copy-start(bf16[1,256,2048]{2,1,0:T(8,128)(2,1)} %param.8) | copy-start | bytes 3145732
  18.9 8.4 %copy-start.3 = (bf16[1,256,2048]{2,1,0:T(8,128)(2,1)S(1)}, bf16[1,256,2048]{2,1,0:T(8,128)(2,1)}, u32[]{:S(2)}) copy-start(bf16[1,256,2048]{2,1,0:T(8,128)(2,1)} %param.13) | copy-start | bytes 3145732
  30.3 15.2 %copy-start.7 = (s32[512]{0:T(512)S(1)}, s32[512]{0:T(512)}, u32[]{:S(2)}) copy-start(s32[512]{0:T(512)} %group_ref.1) | copy-start | bytes 6148
  30.3 28.6 %all-to-all-start.1 = ((bf16[256,4,128]{2,1,0:T(4,128)(2,1)}), bf16[256,4,128]{2,1,0:T(4,128)(2,1)S(1)}, u32[]{:S(2)}, u32[]{:S(2)}) async-start(bf16[256,4,128]{2,1,0:T(4,128)(2,1)} %bitcast.8), calls=%async_computation.1 | async-start | bytes 524288 | tf_op jit(solution)/shard_map/all_to_all | solution.py:327
  51.6 11.5 %copy-start.6 = (bf16[256,512]{1,0:T(8,128)(2,1)S(1)}, bf16[256,512]{1,0:T(8,128)(2,1)}, u32[]{:S(2)}) copy-start(bf16[256,512]{1,0:T(8,128)(2,1)} %get-tuple-element.14._) | copy-start | bytes 786436

commit v3 on v2

--- a/solution.py
+++ b/solution.py
@@ -3,6 +3,7 @@
 
 import jax
 import jax.numpy as jnp
+import numpy as np
 from jax import lax
 from jax.experimental import pallas as pl
 from jax.experimental.pallas import tpu as pltpu
@@ -16,10 +17,34 @@
 HALF = 128
 SCALE = 1.0 / math.sqrt(HD)
 LOG2E = math.log2(math.e)
+PLACES = (4, 4)
+CHIPS = (2, 8)
+LATE_PLACE = (2, 3)
+LATE_CHIP = (0, 4)
 BF16 = jnp.bfloat16
 F32 = jnp.float32
 SMEM = pl.BlockSpec(memory_space=pltpu.SMEM)
 VMEM = pl.BlockSpec(memory_space=pltpu.VMEM)
+
+
+def ring(a, b, size):
+    return min((a - b) % size, (b - a) % size)
+
+
+def hops(a, b, sizes, steps):
+    return sum(ring(i, j, n) * step for i, j, n, step in zip(a, b, sizes, steps))
+
+
+def far_first(sizes, steps, root):
+    members = [(i, j) for i in range(sizes[0]) for j in range(sizes[1])]
+    members.sort(key=lambda m: (m != root, -hops(m, root, sizes, steps)))
+    return [i * sizes[1] + j for i, j in members]
+
+
+PLACE_ORDER = far_first(PLACES, (1, 2), LATE_PLACE)
+CHIP_ORDER = far_first(CHIPS, (1, 1), LATE_CHIP)
+NEAR_ORDER = [c ^ CHIP_ORDER[0] for c in range(len(CHIP_ORDER))]
+FULL_ORDER = [p * len(CHIP_ORDER) + c for p in PLACE_ORDER for c in CHIP_ORDER]
 
 
 def nt_dot(a, b):
@@ -68,16 +93,27 @@
     )
 
 
-def pick_kernel(group_ref, keys_ref, values_ref, out_ref):
+def pick_kernel(
+    group_hbm, keys_hbm, values_hbm, out_ref, group_ref, keys_ref, values_ref, sems
+):
+    copies = [
+        pltpu.make_async_copy(source, target, sems.at[i])
+        for i, (source, target) in enumerate(
+            zip((group_hbm, keys_hbm, values_hbm), (group_ref, keys_ref, values_ref))
+        )
+    ]
+    for copy in copies:
+        copy.start()
+    for copy in copies:
+        copy.wait()
     place_along = lax.axis_index("chip") * CORES + lax.axis_index("core")
-    count = out_ref.shape[0]
-    stride = group_ref.shape[0] // count
-    for p in range(count):
-        owner = group_ref[p * stride + place_along]
+    stride = group_ref.shape[0] // out_ref.shape[0]
+    for i, place in enumerate(PLACE_ORDER):
+        owner = group_ref[place * stride + place_along]
         both = jnp.concatenate(
             [keys_ref[owner].astype(F32), values_ref[owner].astype(F32)], axis=0
         )
-        out_ref[p] = both.astype(BF16)
+        out_ref[i] = both.astype(BF16)
 
 
 def pick(group, keys, values, count):
@@ -85,8 +121,14 @@
     return pl.pallas_call(
         pick_kernel,
         out_shape=jax.ShapeDtypeStruct((count, 2 * rows, width), BF16),
-        in_specs=[SMEM, VMEM, VMEM],
+        in_specs=[pl.BlockSpec(memory_space=pltpu.HBM)] * 3,
         out_specs=VMEM,
+        scratch_shapes=[
+            pltpu.SMEM(group.shape, group.dtype),
+            pltpu.VMEM(keys.shape, keys.dtype),
+            pltpu.VMEM(values.shape, values.dtype),
+            pltpu.SemaphoreType.DMA((3,)),
+        ],
         compiler_params=params(56),
     )(group, keys, values)
 
@@ -265,6 +307,26 @@
     )(length, query, grad, keys, values, front, full)
 
 
+def owners_kernel(rows, group_ref, slots_ref, out_ref):
+    count, size = group_ref.shape[1], slots_ref.shape[1]
+    hit = lax.broadcasted_iota(jnp.int32, (count, size), 0) == slots_ref[...]
+    group = jnp.broadcast_to(group_ref[...].astype(F32).astype(BF16), (8, count))
+    out = nn_dot(group, jnp.where(hit, 1.0, 0.0).astype(BF16))
+    out_ref[...] = out[:1].astype(jnp.int32)
+
+
+def owners_of(group, rows):
+    slots = [m * CORES + core for core in range(CORES) for m in FULL_ORDER]
+    slots = np.repeat(np.array(slots, np.int32), rows)[None]
+    return pl.pallas_call(
+        functools.partial(owners_kernel, rows),
+        out_shape=jax.ShapeDtypeStruct(slots.shape, jnp.int32),
+        in_specs=[VMEM, VMEM],
+        out_specs=VMEM,
+        compiler_params=params(8),
+    )(group[None], slots)
+
+
 def add_kernel(num_prompts, owners_ref, terms_ref, _, out_ref):
     count = terms_ref.shape[0]
     total = out_ref.shape[1]
@@ -287,6 +349,7 @@
 
 
 def place_kernel(parts_ref, key_ref, value_ref):
+    came = [NEAR_ORDER.index(chip) for chip in CHIP_ORDER]
     prompts, own, _ = key_ref.shape
     blocks = parts_ref.shape[0] // (2 * KVH)
     rows = own // blocks
@@ -299,7 +362,9 @@
     for k in range(KVH):
         for side, out_ref in enumerate((key_ref, value_ref)):
             first = (k * 2 + side) * blocks
-            block = parts_ref[first : first + blocks].reshape(size, HD)
+            block = jnp.concatenate(
+                [parts_ref[came[first + w]] for w in range(blocks)], axis=0
+            )
             out_ref[:, :, k * HD : (k + 1) * HD] = nn_dot(move, block).reshape(
                 prompts, own, HD
             )
@@ -315,25 +380,29 @@
     )(parts)
 
 
+def exchange(blocks, axes, order):
+    return lax.all_to_all(blocks, axes, 0, 0, axis_index_groups=[order])
+
+
 def shards(query, resp_keys, resp_values, prompt_keys, prompt_values, out_grad, group, lengths):
     places, chips = lax.axis_size("prompt"), lax.axis_size("chip")
     num_prompts, own, width = prompt_keys.shape
     wanted = pick(group, prompt_keys, prompt_values, places)
-    front = lax.all_to_all(wanted, "prompt", 0, 0)
+    front = exchange(wanted, "prompt", PLACE_ORDER)
     query, grad, keys, values = query[0], out_grad[0], resp_keys[0], resp_values[0]
     stats = own_stats(lengths, query, grad, keys, values)
     front_grad, full = front_part(lengths, query, grad, front, stats)
     rows = 2 * own * width // (chips * HD)
-    terms = lax.all_to_all(
-        front_grad.reshape(places * chips, rows, HD), ("prompt", "chip"), 0, 0
+    terms = exchange(
+        front_grad.reshape(places * chips, rows, HD), ("prompt", "chip"), FULL_ORDER
     )
     query_grad, key_grad, value_grad = rest_part(
         lengths, query, grad, keys, values, front, full
     )
     terms = lax.all_gather(terms, "core", axis=0).reshape(-1, HD)
-    owners = jnp.repeat(jnp.transpose(group.reshape(-1, CORES)).reshape(-1), rows)
-    sums = add_by_prompt(owners[None], terms, key_grad, num_prompts, rows, chips)
-    parts = lax.all_to_all(sums, "chip", 0, 0)
+    owners = owners_of(group, rows)
+    sums = add_by_prompt(owners, terms, key_grad, num_prompts, rows, chips)
+    parts = exchange(sums, "chip", NEAR_ORDER)
     prompt_key_grad, prompt_value_grad = place(parts, prompt_keys.shape)
     return (
         query_grad[None],

time: 75.7 us -> 69.4 us (0.917)
  waiting for transfers between devices: 14.1 us -> 0.21 us
  starting transfers between devices: 28.7 us -> 36.5 us
    all_to_all x2, waiting for transfers between devices: 14.1 us -> 0.21 us  [exchange(): return lax.all_to_all(blocks, axes, 0, 0, axis_index_groups=[order])]
    all_to_all x2, starting transfers between devices: 28.7 us -> 36.5 us  [exchange(): return lax.all_to_all(blocks, axes, 0, 0, axis_index_groups=[order])]
    unnamed x17 -> x18, local copies, waits for them, and re-layouts: 2.47 us -> 2.48 us
  transfers between devices with their start and end apart: 2 -> 2, of which waited for: 2 -> 2; matrix products, arithmetic and copies ran while one was open for 1% -> 0% of each run, Pallas kernels for 9% -> 11%
where the time goes in v3:
time: 69.4 us; the launch traced here: 68.8 us
  starting transfers between devices  36.5 us (53%)
  blocking collectives  15.1 us (22%)
  Pallas kernels  13.1 us (19%)
  local copies, waits for them, and re-layouts  2.48 us (4%)
  between operations  1.38 us (2%)
    all_to_all x2, starting transfers between devices, exchange(): return lax.all_to_all(blocks, axes, 0, 0, axis_index_groups=[order])  36.5 us
    all_to_all x1, blocking collectives, exchange(): return lax.all_to_all(blocks, axes, 0, 0, axis_index_groups=[order])  11.3 us
    pallas_call x1, Pallas kernels, rest_part(): pl.pallas_call(rest_kernel, grid=(KVH,), out_shape=(jax.ShapeDtypeStruct(...  5.52 us
    all_gather x1, blocking collectives, shards(): terms = lax.all_gather(terms, 'core', axis=0).reshape(-1, HD)  3.83 us
    pallas_call x1, Pallas kernels, front_part(): pl.pallas_call(front_kernel, out_shape=(jax.ShapeDtypeStruct((shards_n, K...  2.97 us
    unnamed x18, local copies, waits for them, and re-layouts  2.48 us
    pallas_call x1, Pallas kernels, pick(): pl.pallas_call(pick_kernel, out_shape=jax.ShapeDtypeStruct((count, 2 * ro...  1.62 us
    pallas_call x1, Pallas kernels, own_stats(): pl.pallas_call(own_kernel, out_shape=jax.ShapeDtypeStruct((KVH, rows // H...  1.55 us
  transfers between devices with their start and end apart: 2, of which 2 were waited for; matrix products, arithmetic and copies ran while one was open for 0% of the time, Pallas kernels for 11%

profile of v3, /device:TPU:1, one launch (start us, length us, event | category | flops | bytes accessed | tf_op | source)
XLA Modules:
  0.0 68.8 jit_solution(14205920260602837214)
XLA Ops:
  0.6 1.6 %shard_map.128 = bf16[16,16,512]{2,1,0:T(8,128)(2,1)} custom-call(s32[512]{0:T(512)} %group_hbm.1, bf16[8,8,512]{2,1,0:T(8,128)(2,1)} %keys_hbm.1, bf16[8,8,512]{2,1,0:T(8,128)(2,1)} %values_hbm.1), custom_call_target="tpu_custom_call" | custom-call | tf_op jit(solution)/shard_map/pallas_call | solution.py:121
  2.3 0.0 copy-start.4
  2.3 0.0 copy-start.5
  2.3 15.5 %all-to-all-start = ((bf16[16,16,512]{2,1,0:T(8,128)(2,1)}), bf16[16,16,512]{2,1,0:T(8,128)(2,1)S(1)}, u32[]{:S(2)}, u32[]{:S(2)}) async-start(bf16[16,16,512]{2,1,0:T(8,128)(2,1)} %shard_map.128), calls=%async_computation | async-start | bytes 524288 | tf_op jit(solution)/shard_map/all_to_all | solution.py:384
  18.5 0.0 copy-done.4
  18.5 0.0 copy-done.5
  18.5 0.0 copy-start
  18.5 1.2 %copy-done = bf16[1,256,2048]{2,1,0:T(8,128)(2,1)S(1)} copy-done((bf16[1,256,2048]{2,1,0:T(8,128)(2,1)S(1)}, bf16[1,256,2048]{2,1,0:T(8,128)(2,1)}, u32[]{:S(2)}) %copy-start) | copy-done | bytes 1048600
  19.7 0.0 copy-start.2
  19.7 1.2 %copy-done.2 = bf16[1,256,2048]{2,1,0:T(8,128)(2,1)S(1)} copy-done((bf16[1,256,2048]{2,1,0:T(8,128)(2,1)S(1)}, bf16[1,256,2048]{2,1,0:T(8,128)(2,1)}, u32[]{:S(2)}) %copy-start.2) | copy-done | bytes 1048600
  20.9 0.0 copy-start.1
  20.9 0.0 copy-start.3
  20.9 1.5 %shard_map.129.stats_ref = f32[4,2,8,512]{3,2,1,0:T(8,128)S(1)} custom-call(s32[1]{0:T(128)S(6)} %copy.14.length_ref, bf16[256,2048]{1,0:T(8,128)(2,1)S(1)} %bitcast.10, bf16[256,2048]{1,0:T(8,128)(2,1)S(1)} %bitcast.13, bf16[256,512]{1,0:T(8,128)(2,1)S(1)} %bitcast.17, bf16[256,512]{1,0:T(8,128)(2,1)S(1)} %bitcast.19), custom_call_target="tpu_custom_call" | custom-call | flops 536870912 | bytes 3145728 | tf_op jit(solution)/shard_map/pallas_call | solution.py:267
  22.5 0.2 all-to-all-done.front_ref
  22.6 0.0 copy-done.1
  22.7 0.0 copy-done.3
  22.7 3.0 %shard_map.130 = (bf16[16,4,16,128]{3,2,1,0:T(8,128)(2,1)}, f32[4,2,8,512]{3,2,1,0:T(8,128)S(1)}) custom-call(s32[1]{0:T(128)S(6)} %copy.14.length_ref, bf16[256,2048]{1,0:T(8,128)(2,1)S(1)} %bitcast.11, bf16[256,2048]{1,0:T(8,128)(2,1)S(1)} %bitcast.14, bf16[16,16,512]{2,1,0:T(8,128)(2,1)S(1)} %all-to-all-done.front_ref, ...), custom_call_target="tpu_custom_call" | custom-call | flops 536870912 | bytes 3145728 | tf_op jit(solution)/shard_map/pallas_call | solution.py:279
  25.6 0.0 copy-start.7
  25.6 0.0 copy-start.8
  25.6 21.0 %all-to-all-start.1 = ((bf16[256,4,128]{2,1,0:T(4,128)(2,1)}), bf16[256,4,128]{2,1,0:T(4,128)(2,1)S(1)}, u32[]{:S(2)}, u32[]{:S(2)}) async-start(bf16[256,4,128]{2,1,0:T(4,128)(2,1)} %bitcast.8), calls=%async_computation.1 | async-start | bytes 524288 | tf_op jit(solution)/shard_map/all_to_all | solution.py:384
  46.6 0.0 copy-done.7
  46.6 0.0 copy-done.8
  46.6 0.4 shard_map.132.owners_ref
  47.0 5.5 %shard_map.131 = (bf16[256,2048]{1,0:T(8,128)(2,1)}, bf16[256,512]{1,0:T(8,128)(2,1)}, bf16[256,512]{1,0:T(8,128)(2,1)}) custom-call(s32[1]{0:T(128)S(6)} %copy.14.length_ref, bf16[256,2048]{1,0:T(8,128)(2,1)S(1)} %bitcast.12, bf16[256,2048]{1,0:T(8,128)(2,1)S(1)} %bitcast.15, bf16[256,512]{1,0:T(8,128)(2,1)S(1)} %bitcast.18, bf16[256,512]{1,0:T(8,128)(2,1)S(1)} %bitcast.20, ...), custom_call_target="tpu_custom_call" | custom-call | flops 2013265920 | bytes 3145728 | tf_op jit(solution)/shard_map/pallas_call | solution.py:295
  52.5 0.0 copy-start.6
  52.5 0.1 all-to-all-done.1
  52.6 3.8 %all-gather = bf16[512,4,128]{2,1,0:T(4,128)(2,1)S(1)} all-gather(bf16[256,4,128]{2,1,0:T(4,128)(2,1)S(1)} %all-to-all-done.1), channel_id=2, replica_groups=mesh['prompt'=16,'chip'=16,'core'=2] {'core'}, dimensions={0}, use_global_device_ids=true | all-gather | bytes 786432 | tf_op jit(solution)/shard_map/all_gather | solution.py:402
  56.4 0.0 copy-done.6
  56.4 0.2 shard_map.133
  56.7 11.3 %all_to_all.15.parts_ref = bf16[16,32,128]{2,1,0:T(8,128)(2,1)S(1)} all-to-all(bf16[16,32,128]{2,1,0:T(8,128)(2,1)S(1)} %shard_map.133), channel_id=1, replica_groups={{8,10,12,14,0,2,4,6,24,26,28,30,16,18,20,22},{9,11,13,15,1,3,5,7,25,27,..., dimensions={0} | all-to-all | bytes 262144 | tf_op jit(solution)/shard_map/all_to_all | solution.py:384
  67.9 0.9 %shard_map.134 = (f32[8,8,512]{2,1,0:T(8,128)}, f32[8,8,512]{2,1,0:T(8,128)}) custom-call(bf16[16,32,128]{2,1,0:T(8,128)(2,1)S(1)} %all_to_all.15.parts_ref), custom_call_target="tpu_custom_call" | custom-call | tf_op jit(solution)/shard_map/pallas_call | solution.py:374
Async XLA Ops:
  2.3 16.2 %copy-start.4 = (bf16[1,256,512]{2,1,0:T(8,128)(2,1)S(1)}, bf16[1,256,512]{2,1,0:T(8,128)(2,1)}, u32[]{:S(2)}) copy-start(bf16[1,256,512]{2,1,0:T(8,128)(2,1)} %param.10) | copy-start | bytes 786436
  2.3 16.2 %copy-start.5 = (bf16[1,256,512]{2,1,0:T(8,128)(2,1)S(1)}, bf16[1,256,512]{2,1,0:T(8,128)(2,1)}, u32[]{:S(2)}) copy-start(bf16[1,256,512]{2,1,0:T(8,128)(2,1)} %param.11) | copy-start | bytes 786436
  2.3 20.4 %all-to-all-start = ((bf16[16,16,512]{2,1,0:T(8,128)(2,1)}), bf16[16,16,512]{2,1,0:T(8,128)(2,1)S(1)}, u32[]{:S(2)}, u32[]{:S(2)}) async-start(bf16[16,16,512]{2,1,0:T(8,128)(2,1)} %shard_map.128), calls=%async_computation | async-start | bytes 524288 | tf_op jit(solution)/shard_map/all_to_all | solution.py:384
  18.5 1.2 %copy-start = (bf16[1,256,2048]{2,1,0:T(8,128)(2,1)S(1)}, bf16[1,256,2048]{2,1,0:T(8,128)(2,1)}, u32[]{:S(2)}) copy-start(bf16[1,256,2048]{2,1,0:T(8,128)(2,1)} %param.9) | copy-start | bytes 3145732
  19.7 1.2 %copy-start.2 = (bf16[1,256,2048]{2,1,0:T(8,128)(2,1)S(1)}, bf16[1,256,2048]{2,1,0:T(8,128)(2,1)}, u32[]{:S(2)}) copy-start(bf16[1,256,2048]{2,1,0:T(8,128)(2,1)} %param.14) | copy-start | bytes 3145732
  20.9 1.7 %copy-start.1 = (bf16[1,256,2048]{2,1,0:T(8,128)(2,1)S(1)}, bf16[1,256,2048]{2,1,0:T(8,128)(2,1)}, u32[]{:S(2)}) copy-start(bf16[1,256,2048]{2,1,0:T(8,128)(2,1)} %param.9) | copy-start | bytes 3145732
  20.9 1.7 %copy-start.3 = (bf16[1,256,2048]{2,1,0:T(8,128)(2,1)S(1)}, bf16[1,256,2048]{2,1,0:T(8,128)(2,1)}, u32[]{:S(2)}) copy-start(bf16[1,256,2048]{2,1,0:T(8,128)(2,1)} %param.14) | copy-start | bytes 3145732
  25.6 21.0 %copy-start.7 = (s32[512]{0:T(512)S(1)}, s32[512]{0:T(512)}, u32[]{:S(2)}) copy-start(s32[512]{0:T(512)} %group_hbm.1) | copy-start | bytes 6148
  25.6 21.0 %copy-start.8 = (s32[1,2048]{1,0:T(1,128)S(1)}, s32[1,2048]{1,0:T(1,128)}, u32[]{:S(2)}) copy-start(s32[1,2048]{1,0:T(1,128)} %constant.2.clone.slots_ref) | copy-start | bytes 24580
  25.6 27.0 %all-to-all-start.1 = ((bf16[256,4,128]{2,1,0:T(4,128)(2,1)}), bf16[256,4,128]{2,1,0:T(4,128)(2,1)S(1)}, u32[]{:S(2)}, u32[]{:S(2)}) async-start(bf16[256,4,128]{2,1,0:T(4,128)(2,1)} %bitcast.8), calls=%async_computation.1 | async-start | bytes 524288 | tf_op jit(solution)/shard_map/all_to_all | solution.py:384
  52.5 3.9 %copy-start.6 = (bf16[256,512]{1,0:T(8,128)(2,1)S(1)}, bf16[256,512]{1,0:T(8,128)(2,1)}, u32[]{:S(2)}) copy-start(bf16[256,512]{1,0:T(8,128)(2,1)} %get-tuple-element.14._) | copy-start | bytes 786436

commit v4 on v3

--- a/solution.py
+++ b/solution.py
@@ -19,12 +19,13 @@
 LOG2E = math.log2(math.e)
 PLACES = (4, 4)
 CHIPS = (2, 8)
-LATE_PLACE = (2, 3)
+LATE_PLACE = (2, 2)
 LATE_CHIP = (0, 4)
 BF16 = jnp.bfloat16
 F32 = jnp.float32
 SMEM = pl.BlockSpec(memory_space=pltpu.SMEM)
 VMEM = pl.BlockSpec(memory_space=pltpu.VMEM)
+HBM = pl.BlockSpec(memory_space=pltpu.HBM)
 
 
 def ring(a, b, size):
@@ -91,6 +92,19 @@
         keys.reshape(shards_n * both // 2, HD).astype(BF16),
         values.reshape(shards_n * both // 2, HD).astype(BF16),
     )
+
+
+def peer_chip(side, row, place):
+    bent = place % PLACES[1] >= PLACES[1] // 2
+    return (1 - side if bent else side) * CHIPS[1] + row
+
+
+def front_groups():
+    return [
+        [place * len(CHIP_ORDER) + peer_chip(side, row, place) for place in PLACE_ORDER]
+        for side in range(CHIPS[0])
+        for row in range(CHIPS[1])
+    ]
 
 
 def pick_kernel(
@@ -104,12 +118,15 @@
     ]
     for copy in copies:
         copy.start()
+    chip, core = lax.axis_index("chip"), lax.axis_index("core")
+    row = chip % CHIPS[1]
+    bent = lax.axis_index("prompt") % PLACES[1] >= PLACES[1] // 2
+    side = jnp.where(bent, 1 - chip // CHIPS[1], chip // CHIPS[1])
     for copy in copies:
         copy.wait()
-    place_along = lax.axis_index("chip") * CORES + lax.axis_index("core")
-    stride = group_ref.shape[0] // out_ref.shape[0]
     for i, place in enumerate(PLACE_ORDER):
-        owner = group_ref[place * stride + place_along]
+        peer = place * len(CHIP_ORDER) + peer_chip(side, row, place)
+        owner = group_ref[peer * CORES + core]
         both = jnp.concatenate(
             [keys_ref[owner].astype(F32), values_ref[owner].astype(F32)], axis=0
         )
@@ -121,7 +138,7 @@
     return pl.pallas_call(
         pick_kernel,
         out_shape=jax.ShapeDtypeStruct((count, 2 * rows, width), BF16),
-        in_specs=[pl.BlockSpec(memory_space=pltpu.HBM)] * 3,
+        in_specs=[HBM] * 3,
         out_specs=VMEM,
         scratch_shapes=[
             pltpu.SMEM(group.shape, group.dtype),
@@ -133,7 +150,17 @@
     )(group, keys, values)
 
 
-def own_kernel(length_ref, query_ref, grad_ref, keys_ref, values_ref, stats_ref):
+def own_kernel(
+    length_ref,
+    query_ref,
+    grad_ref,
+    keys_ref,
+    values_ref,
+    group_ref,
+    slots_ref,
+    stats_ref,
+    owners_ref,
+):
     length = length_ref[0]
     for k in range(KVH):
         features = slice(k * HD, (k + 1) * HD)
@@ -149,45 +176,83 @@
             dot = jnp.sum(weights * dprob, axis=0, keepdims=True)
             fill = jnp.zeros((5, top.shape[1]), F32)
             stats_ref[k, half] = jnp.concatenate([top, total, dot, fill], axis=0)
+    count, size = group_ref.shape[1], slots_ref.shape[1]
+    hit = lax.broadcasted_iota(jnp.int32, (count, size), 0) == slots_ref[...]
+    group = jnp.broadcast_to(group_ref[...].astype(F32).astype(BF16), (8, count))
+    owners = nn_dot(group, jnp.where(hit, 1.0, 0.0).astype(BF16))
+    owners_ref[...] = owners[:1].astype(jnp.int32)
 
 
 def front_kernel(
-    length_ref, query_ref, grad_ref, front_ref, stats_ref, front_grad_ref, full_ref
+    length_ref,
+    query_ref,
+    grad_ref,
+    front_ref,
+    stats_ref,
+    front_grad_hbm,
+    full_ref,
+    front_grad_ref,
+    sems,
 ):
     length = length_ref[0]
-    shards_n, _, both, _ = front_grad_ref.shape
+    _, shards_n, both, _ = front_grad_ref.shape
+    copies = [
+        pltpu.make_async_copy(front_grad_ref.at[k], front_grad_hbm.at[:, k], sems.at[k])
+        for k in range(KVH)
+    ]
+    front_len = shards_n * (both // 2)
+    halves = range(query_ref.shape[0] // HALF)
+
+    def begin(k):
+        keys, values = front_parts(front_ref, k)
+        query = jnp.concatenate([stack_heads(query_ref, half, k) for half in halves])
+        grad = jnp.concatenate(
+            [live_grad(grad_ref, length, half, k) for half in halves]
+        )
+        both = jnp.concatenate([query, grad], axis=1)
+        none = jnp.zeros_like(keys)
+        front = jnp.concatenate(
+            [
+                jnp.concatenate([keys, none], axis=1),
+                jnp.concatenate([none, values], axis=1),
+            ]
+        )
+        return both, nt_dot(front, both)
+
+    ahead = begin(0)
     for k in range(KVH):
-        keys, values = front_parts(front_ref, k)
-        key_total, value_total = 0.0, 0.0
-        for half in range(query_ref.shape[0] // HALF):
-            query = stack_heads(query_ref, half, k)
-            grad = live_grad(grad_ref, length, half, k)
-            stats = stats_ref[k, half]
-            own_top, own_total, own_dot = stats[0:1], stats[1:2], stats[2:3]
-            scores = nt_dot(keys, query)
-            top = jnp.maximum(jnp.max(scores, axis=0, keepdims=True), own_top)
-            weights = exp_scaled(scores - top)
-            rescale = exp_scaled(own_top - top)
-            total = jnp.sum(weights, axis=0, keepdims=True) + own_total * rescale
-            inverse = 1.0 / total
-            prob = weights * inverse
-            prob_low = prob.astype(BF16)
-            dprob = nt_dot(values, grad)
-            delta = jnp.sum(prob * dprob, axis=0, keepdims=True) + own_dot * (
-                rescale * inverse
-            )
-            dscore = (prob * (dprob - delta)).astype(BF16)
-            key_total = key_total + nn_dot(dscore, query)
-            value_total = value_total + nn_dot(prob_low, grad)
-            fill = jnp.zeros((5, top.shape[1]), F32)
-            full_ref[k, half] = jnp.concatenate([top, inverse, delta, fill], axis=0)
-        front_grad_ref[:, k] = jnp.concatenate(
+        rows, dots = ahead
+        if k + 1 < KVH:
+            ahead = begin(k + 1)
+        scores, dprob = dots[:front_len], dots[front_len:]
+        stats = jnp.concatenate([stats_ref[k, half] for half in halves], axis=1)
+        own_top, own_total, own_dot = stats[0:1], stats[1:2], stats[2:3]
+        top = jnp.maximum(jnp.max(scores, axis=0, keepdims=True), own_top)
+        weights = exp_scaled(scores - top)
+        rescale = exp_scaled(own_top - top)
+        total = jnp.sum(weights, axis=0, keepdims=True) + own_total * rescale
+        inverse = 1.0 / total
+        prob = weights * inverse
+        dots = jnp.sum(weights * dprob, axis=0, keepdims=True) + own_dot * rescale
+        delta = dots * inverse
+        dscore = (prob * (dprob - delta)).astype(BF16)
+        sums = nn_dot(jnp.concatenate([dscore, prob.astype(BF16)]), rows)
+        key_total = sums[:front_len, :HD] * SCALE
+        value_total = sums[front_len:, HD:]
+        fill = jnp.zeros((5, top.shape[1]), F32)
+        full = jnp.concatenate([top, inverse, delta, fill], axis=0)
+        for half in halves:
+            full_ref[k, half] = full[:, half * GROUP * HALF : (half + 1) * GROUP * HALF]
+        front_grad_ref[k] = jnp.concatenate(
             [
-                (key_total * SCALE).reshape(shards_n, both // 2, HD),
+                key_total.reshape(shards_n, both // 2, HD),
                 value_total.reshape(shards_n, both // 2, HD),
             ],
             axis=1,
         ).astype(BF16)
+        copies[k].start()
+    for copy in copies:
+        copy.wait()
 
 
 def rest_kernel(
@@ -262,16 +327,21 @@
     )
 
 
-def own_stats(length, query, grad, keys, values):
+def own_stats(length, query, grad, keys, values, group, copies):
     rows = query.shape[0]
+    slots = [m * CORES + core for core in range(CORES) for m in FULL_ORDER]
+    slots = np.repeat(np.array(slots, np.int32), copies)[None]
     return pl.pallas_call(
         own_kernel,
-        out_shape=jax.ShapeDtypeStruct((KVH, rows // HALF, 8, GROUP * HALF), F32),
-        in_specs=[SMEM, VMEM, VMEM, VMEM, VMEM],
-        out_specs=VMEM,
+        out_shape=(
+            jax.ShapeDtypeStruct((KVH, rows // HALF, 8, GROUP * HALF), F32),
+            jax.ShapeDtypeStruct(slots.shape, jnp.int32),
+        ),
+        in_specs=[SMEM] + [VMEM] * 6,
+        out_specs=(VMEM, VMEM),
         compiler_params=params(16),
         cost_estimate=cost(2, 256),
-    )(length, query, grad, keys, values)
+    )(length, query, grad, keys, values, group[None], slots)
 
 
 def front_part(length, query, grad, front, own):
@@ -283,7 +353,11 @@
             jax.ShapeDtypeStruct(own.shape, F32),
         ),
         in_specs=[SMEM, VMEM, VMEM, VMEM, VMEM],
-        out_specs=(VMEM, VMEM),
+        out_specs=(HBM, VMEM),
+        scratch_shapes=[
+            pltpu.VMEM((KVH, shards_n, both, HD), BF16),
+            pltpu.SemaphoreType.DMA((KVH,)),
+        ],
         compiler_params=params(16),
         cost_estimate=cost(4, 128),
     )(length, query, grad, front, own)
@@ -307,26 +381,6 @@
     )(length, query, grad, keys, values, front, full)
 
 
-def owners_kernel(rows, group_ref, slots_ref, out_ref):
-    count, size = group_ref.shape[1], slots_ref.shape[1]
-    hit = lax.broadcasted_iota(jnp.int32, (count, size), 0) == slots_ref[...]
-    group = jnp.broadcast_to(group_ref[...].astype(F32).astype(BF16), (8, count))
-    out = nn_dot(group, jnp.where(hit, 1.0, 0.0).astype(BF16))
-    out_ref[...] = out[:1].astype(jnp.int32)
-
-
-def owners_of(group, rows):
-    slots = [m * CORES + core for core in range(CORES) for m in FULL_ORDER]
-    slots = np.repeat(np.array(slots, np.int32), rows)[None]
-    return pl.pallas_call(
-        functools.partial(owners_kernel, rows),
-        out_shape=jax.ShapeDtypeStruct(slots.shape, jnp.int32),
-        in_specs=[VMEM, VMEM],
-        out_specs=VMEM,
-        compiler_params=params(8),
-    )(group[None], slots)
-
-
 def add_kernel(num_prompts, owners_ref, terms_ref, _, out_ref):
     count = terms_ref.shape[0]
     total = out_ref.shape[1]
@@ -348,9 +402,9 @@
     )(owners, terms, after)
 
 
-def place_kernel(parts_ref, key_ref, value_ref):
+def place_kernel(parts_ref, key_hbm, value_hbm, out_ref, sems):
     came = [NEAR_ORDER.index(chip) for chip in CHIP_ORDER]
-    prompts, own, _ = key_ref.shape
+    _, prompts, own, _ = out_ref.shape
     blocks = parts_ref.shape[0] // (2 * KVH)
     rows = own // blocks
     size = prompts * own
@@ -359,15 +413,20 @@
     prompt, row = to // own, to % own
     hit = at == (row // rows) * (rows * prompts) + prompt * rows + row % rows
     move = jnp.where(hit, 1.0, 0.0).astype(BF16)
-    for k in range(KVH):
-        for side, out_ref in enumerate((key_ref, value_ref)):
+    copies = []
+    for side, out_hbm in enumerate((key_hbm, value_hbm)):
+        for k in range(KVH):
             first = (k * 2 + side) * blocks
             block = jnp.concatenate(
                 [parts_ref[came[first + w]] for w in range(blocks)], axis=0
             )
-            out_ref[:, :, k * HD : (k + 1) * HD] = nn_dot(move, block).reshape(
+            out_ref[side, :, :, k * HD : (k + 1) * HD] = nn_dot(move, block).reshape(
                 prompts, own, HD
             )
+        copies.append(pltpu.make_async_copy(out_ref.at[side], out_hbm, sems.at[side]))
+        copies[-1].start()
+    for copy in copies:
+        copy.wait()
 
 
 def place(parts, shape):
@@ -375,34 +434,37 @@
         place_kernel,
         out_shape=(jax.ShapeDtypeStruct(shape, F32), jax.ShapeDtypeStruct(shape, F32)),
         in_specs=[VMEM],
-        out_specs=(VMEM, VMEM),
+        out_specs=(HBM, HBM),
+        scratch_shapes=[
+            pltpu.VMEM((2,) + shape, F32),
+            pltpu.SemaphoreType.DMA((2,)),
+        ],
         compiler_params=params(4),
     )(parts)
 
 
-def exchange(blocks, axes, order):
-    return lax.all_to_all(blocks, axes, 0, 0, axis_index_groups=[order])
+def exchange(blocks, axes, groups):
+    return lax.all_to_all(blocks, axes, 0, 0, axis_index_groups=groups)
 
 
 def shards(query, resp_keys, resp_values, prompt_keys, prompt_values, out_grad, group, lengths):
     places, chips = lax.axis_size("prompt"), lax.axis_size("chip")
     num_prompts, own, width = prompt_keys.shape
     wanted = pick(group, prompt_keys, prompt_values, places)
-    front = exchange(wanted, "prompt", PLACE_ORDER)
+    front = exchange(wanted, ("prompt", "chip"), front_groups())
     query, grad, keys, values = query[0], out_grad[0], resp_keys[0], resp_values[0]
-    stats = own_stats(lengths, query, grad, keys, values)
+    rows = 2 * own * width // (chips * HD)
+    stats, owners = own_stats(lengths, query, grad, keys, values, group, rows)
     front_grad, full = front_part(lengths, query, grad, front, stats)
-    rows = 2 * own * width // (chips * HD)
     terms = exchange(
-        front_grad.reshape(places * chips, rows, HD), ("prompt", "chip"), FULL_ORDER
+        front_grad.reshape(places * chips, rows, HD), ("prompt", "chip"), [FULL_ORDER]
     )
     query_grad, key_grad, value_grad = rest_part(
         lengths, query, grad, keys, values, front, full
     )
     terms = lax.all_gather(terms, "core", axis=0).reshape(-1, HD)
-    owners = owners_of(group, rows)
     sums = add_by_prompt(owners, terms, key_grad, num_prompts, rows, chips)
-    parts = exchange(sums, "chip", NEAR_ORDER)
+    parts = exchange(sums, "chip", [NEAR_ORDER])
     prompt_key_grad, prompt_value_grad = place(parts, prompt_keys.shape)
     return (
         query_grad[None],

time: 69.4 us -> 67.9 us (0.978)
  starting transfers between devices: 36.5 us -> 34.4 us
    all_to_all x2, starting transfers between devices: 36.5 us -> 34.4 us  [exchange(): return lax.all_to_all(blocks, axes, 0, 0, axis_index_groups=groups)]
    pallas_call x2 -> x1, Pallas kernels: 1.94 us -> 2.03 us  [own_stats(): pl.pallas_call(own_kernel, out_shape=(jax.ShapeDtypeStruct((KVH, rows //...]
  transfers between devices with their start and end apart: 2 -> 2, of which waited for: 2 -> 1; matrix products, arithmetic and copies ran while one was open for 0% -> 0% of each run, Pallas kernels for 11% -> 11%
where the time goes in v4:
time: 67.9 us; the launch traced here: 67.4 us
  starting transfers between devices  34.4 us (51%)
  blocking collectives  15.4 us (23%)
  Pallas kernels  12.8 us (19%)
  local copies, waits for them, and re-layouts  3.12 us (5%)
  between operations  1.39 us (2%)
    all_to_all x2, starting transfers between devices, exchange(): return lax.all_to_all(blocks, axes, 0, 0, axis_index_groups=groups)  34.4 us
    all_to_all x1, blocking collectives, exchange(): return lax.all_to_all(blocks, axes, 0, 0, axis_index_groups=groups)  11.6 us
    pallas_call x1, Pallas kernels, rest_part(): pl.pallas_call(rest_kernel, grid=(KVH,), out_shape=(jax.ShapeDtypeStruct(...  5.56 us
    all_gather x1, blocking collectives, shards(): terms = lax.all_gather(terms, 'core', axis=0).reshape(-1, HD)  3.81 us
    unnamed x18, local copies, waits for them, and re-layouts  3.12 us
    pallas_call x1, Pallas kernels, front_part(): pl.pallas_call(front_kernel, out_shape=(jax.ShapeDtypeStruct((shards_n, K...  2.53 us
    pallas_call x1, Pallas kernels, own_stats(): pl.pallas_call(own_kernel, out_shape=(jax.ShapeDtypeStruct((KVH, rows //...  2.03 us
    pallas_call x1, Pallas kernels, pick(): pl.pallas_call(pick_kernel, out_shape=jax.ShapeDtypeStruct((count, 2 * ro...  1.62 us
  transfers between devices with their start and end apart: 2, of which 1 were waited for; matrix products, arithmetic and copies ran while one was open for 0% of the time, Pallas kernels for 11%

profile of v4, /device:TPU:1, one launch (start us, length us, event | category | flops | bytes accessed | tf_op | source)
XLA Modules:
  0.0 67.4 jit_solution(4430606777172603709)
XLA Ops:
  0.6 1.6 %shard_map.128 = bf16[16,16,512]{2,1,0:T(8,128)(2,1)} custom-call(s32[512]{0:T(512)} %group_hbm.1, bf16[8,8,512]{2,1,0:T(8,128)(2,1)} %keys_hbm.1, bf16[8,8,512]{2,1,0:T(8,128)(2,1)} %values_hbm.1), custom_call_target="tpu_custom_call" | custom-call | tf_op jit(solution)/shard_map/pallas_call | solution.py:138
  2.3 0.0 copy-start.4
  2.3 0.0 copy-start.5
  2.3 16.2 %all-to-all-start = ((bf16[16,16,512]{2,1,0:T(8,128)(2,1)}), bf16[16,16,512]{2,1,0:T(8,128)(2,1)S(1)}, u32[]{:S(2)}, u32[]{:S(2)}) async-start(bf16[16,16,512]{2,1,0:T(8,128)(2,1)} %shard_map.128), calls=%async_computation | async-start | bytes 524288 | tf_op jit(solution)/shard_map/all_to_all | solution.py:447
  18.5 0.0 copy-start.7
  19.1 0.0 copy-start.8
  19.2 0.0 copy-done.4
  19.2 0.0 copy-done.5
  19.2 0.0 copy-done.7
  19.2 0.6 copy-done.8
  19.8 0.0 copy-start
  19.8 1.2 %copy-done = bf16[1,256,2048]{2,1,0:T(8,128)(2,1)S(1)} copy-done((bf16[1,256,2048]{2,1,0:T(8,128)(2,1)S(1)}, bf16[1,256,2048]{2,1,0:T(8,128)(2,1)}, u32[]{:S(2)}) %copy-start) | copy-done | bytes 1048600
  21.1 0.0 copy-start.2
  21.1 1.2 %copy-done.2 = bf16[1,256,2048]{2,1,0:T(8,128)(2,1)S(1)} copy-done((bf16[1,256,2048]{2,1,0:T(8,128)(2,1)S(1)}, bf16[1,256,2048]{2,1,0:T(8,128)(2,1)}, u32[]{:S(2)}) %copy-start.2) | copy-done | bytes 1048600
  22.3 0.0 copy-start.1
  22.3 0.0 copy-start.3
  22.3 2.0 %shard_map.129 = (f32[4,2,8,512]{3,2,1,0:T(8,128)S(1)}, s32[1,2048]{1,0:T(1,128)S(1)}) custom-call(s32[1]{0:T(128)S(6)} %copy.14.length_ref, bf16[256,2048]{1,0:T(8,128)(2,1)S(1)} %bitcast.10, bf16[256,2048]{1,0:T(8,128)(2,1)S(1)} %bitcast.13, bf16[256,512]{1,0:T(8,128)(2,1)S(1)} %bitcast.17, bf16[256,512]{1,0:T(8,128)(2,1)S(1)} %bitcast.19, ...), custom_call_target="tpu_custom_call" | custom-call | flops 536870912 | bytes 3145728 | tf_op jit(solution)/shard_map/pallas_call | solution.py:334
  24.3 0.4 all-to-all-done.front_ref
  24.7 0.0 copy-done.1
  24.7 0.0 copy-done.3
  24.7 2.5 %shard_map.130 = (bf16[16,4,16,128]{3,2,1,0:T(8,128)(2,1)}, f32[4,2,8,512]{3,2,1,0:T(8,128)S(1)}) custom-call(s32[1]{0:T(128)S(6)} %copy.14.length_ref, bf16[256,2048]{1,0:T(8,128)(2,1)S(1)} %bitcast.11, bf16[256,2048]{1,0:T(8,128)(2,1)S(1)} %bitcast.14, bf16[16,16,512]{2,1,0:T(8,128)(2,1)S(1)} %all-to-all-done.front_ref, ...), custom_call_target="tpu_custom_call" | custom-call | flops 536870912 | bytes 3145728 | tf_op jit(solution)/shard_map/pallas_call | solution.py:349
  27.2 18.2 %all-to-all-start.1 = ((bf16[256,4,128]{2,1,0:T(4,128)(2,1)}), bf16[256,4,128]{2,1,0:T(4,128)(2,1)S(1)}, u32[]{:S(2)}, u32[]{:S(2)}) async-start(bf16[256,4,128]{2,1,0:T(4,128)(2,1)} %bitcast.8), calls=%async_computation.1 | async-start | bytes 524288 | tf_op jit(solution)/shard_map/all_to_all | solution.py:447
  45.4 5.6 %shard_map.131 = (bf16[256,2048]{1,0:T(8,128)(2,1)}, bf16[256,512]{1,0:T(8,128)(2,1)}, bf16[256,512]{1,0:T(8,128)(2,1)}) custom-call(s32[1]{0:T(128)S(6)} %copy.14.length_ref, bf16[256,2048]{1,0:T(8,128)(2,1)S(1)} %bitcast.12, bf16[256,2048]{1,0:T(8,128)(2,1)S(1)} %bitcast.15, bf16[256,512]{1,0:T(8,128)(2,1)S(1)} %bitcast.18, bf16[256,512]{1,0:T(8,128)(2,1)S(1)} %bitcast.20, ...), custom_call_target="tpu_custom_call" | custom-call | flops 2013265920 | bytes 3145728 | tf_op jit(solution)/shard_map/pallas_call | solution.py:369
  51.0 0.0 copy-start.6
  51.0 0.0 all-to-all-done.1
  51.0 3.8 %all-gather = bf16[512,4,128]{2,1,0:T(4,128)(2,1)S(1)} all-gather(bf16[256,4,128]{2,1,0:T(4,128)(2,1)S(1)} %all-to-all-done.1), channel_id=2, replica_groups=mesh['prompt'=16,'chip'=16,'core'=2] {'core'}, dimensions={0}, use_global_device_ids=true | all-gather | bytes 786432 | tf_op jit(solution)/shard_map/all_gather | solution.py:465
  54.8 0.0 copy-done.6
  54.8 0.2 shard_map.132
  55.0 11.6 %all_to_all.15.parts_ref = bf16[16,32,128]{2,1,0:T(8,128)(2,1)S(1)} all-to-all(bf16[16,32,128]{2,1,0:T(8,128)(2,1)S(1)} %shard_map.132), channel_id=1, replica_groups={{8,10,12,14,0,2,4,6,24,26,28,30,16,18,20,22},{9,11,13,15,1,3,5,7,25,27,..., dimensions={0} | all-to-all | bytes 262144 | tf_op jit(solution)/shard_map/all_to_all | solution.py:447
  66.6 0.9 %shard_map.133 = (f32[8,8,512]{2,1,0:T(8,128)}, f32[8,8,512]{2,1,0:T(8,128)}) custom-call(bf16[16,32,128]{2,1,0:T(8,128)(2,1)S(1)} %all_to_all.15.parts_ref), custom_call_target="tpu_custom_call" | custom-call | tf_op jit(solution)/shard_map/pallas_call | solution.py:433
Async XLA Ops:
  2.3 16.9 %copy-start.4 = (bf16[1,256,512]{2,1,0:T(8,128)(2,1)S(1)}, bf16[1,256,512]{2,1,0:T(8,128)(2,1)}, u32[]{:S(2)}) copy-start(bf16[1,256,512]{2,1,0:T(8,128)(2,1)} %param.10) | copy-start | bytes 786436
  2.3 16.9 %copy-start.5 = (bf16[1,256,512]{2,1,0:T(8,128)(2,1)S(1)}, bf16[1,256,512]{2,1,0:T(8,128)(2,1)}, u32[]{:S(2)}) copy-start(bf16[1,256,512]{2,1,0:T(8,128)(2,1)} %param.11) | copy-start | bytes 786436
  2.3 22.4 %all-to-all-start = ((bf16[16,16,512]{2,1,0:T(8,128)(2,1)}), bf16[16,16,512]{2,1,0:T(8,128)(2,1)S(1)}, u32[]{:S(2)}, u32[]{:S(2)}) async-start(bf16[16,16,512]{2,1,0:T(8,128)(2,1)} %shard_map.128), calls=%async_computation | async-start | bytes 524288 | tf_op jit(solution)/shard_map/all_to_all | solution.py:447
  18.5 0.7 %copy-start.7 = (s32[1,2048]{1,0:T(1,128)S(1)}, s32[1,2048]{1,0:T(1,128)}, u32[]{:S(2)}) copy-start(s32[1,2048]{1,0:T(1,128)} %constant.2.clone.slots_ref) | copy-start | bytes 24580
  19.1 0.7 %copy-start.8 = (s32[512]{0:T(512)S(1)}, s32[512]{0:T(512)}, u32[]{:S(2)}) copy-start(s32[512]{0:T(512)} %group_hbm.1) | copy-start | bytes 6148
  19.8 1.2 %copy-start = (bf16[1,256,2048]{2,1,0:T(8,128)(2,1)S(1)}, bf16[1,256,2048]{2,1,0:T(8,128)(2,1)}, u32[]{:S(2)}) copy-start(bf16[1,256,2048]{2,1,0:T(8,128)(2,1)} %param.9) | copy-start | bytes 3145732
  21.1 1.2 %copy-start.2 = (bf16[1,256,2048]{2,1,0:T(8,128)(2,1)S(1)}, bf16[1,256,2048]{2,1,0:T(8,128)(2,1)}, u32[]{:S(2)}) copy-start(bf16[1,256,2048]{2,1,0:T(8,128)(2,1)} %param.14) | copy-start | bytes 3145732
  22.3 2.4 %copy-start.1 = (bf16[1,256,2048]{2,1,0:T(8,128)(2,1)S(1)}, bf16[1,256,2048]{2,1,0:T(8,128)(2,1)}, u32[]{:S(2)}) copy-start(bf16[1,256,2048]{2,1,0:T(8,128)(2,1)} %param.9) | copy-start | bytes 3145732
  22.3 2.4 %copy-start.3 = (bf16[1,256,2048]{2,1,0:T(8,128)(2,1)S(1)}, bf16[1,256,2048]{2,1,0:T(8,128)(2,1)}, u32[]{:S(2)}) copy-start(bf16[1,256,2048]{2,1,0:T(8,128)(2,1)} %param.14) | copy-start | bytes 3145732
  27.2 23.7 %all-to-all-start.1 = ((bf16[256,4,128]{2,1,0:T(4,128)(2,1)}), bf16[256,4,128]{2,1,0:T(4,128)(2,1)S(1)}, u32[]{:S(2)}, u32[]{:S(2)}) async-start(bf16[256,4,128]{2,1,0:T(4,128)(2,1)} %bitcast.8), calls=%async_computation.1 | async-start | bytes 524288 | tf_op jit(solution)/shard_map/all_to_all | solution.py:447
  51.0 3.8 %copy-start.6 = (bf16[256,512]{1,0:T(8,128)(2,1)S(1)}, bf16[256,512]{1,0:T(8,128)(2,1)}, u32[]{:S(2)}) copy-start(bf16[256,512]{1,0:T(8,128)(2,1)} %get-tuple-element.17._) | copy-start | bytes 786436

commit v5 on v4

--- a/solution.py
+++ b/solution.py
@@ -266,7 +266,9 @@
     query_grad_ref,
     key_grad_ref,
     value_grad_ref,
+    done_ref,
 ):
+    done_ref[...] = jnp.zeros_like(done_ref)
     length = length_ref[0]
     front_keys, front_values = front_parts(front_ref)
     front_len = front_keys.shape[0]
@@ -373,9 +375,10 @@
             jax.ShapeDtypeStruct(query.shape, BF16),
             jax.ShapeDtypeStruct(keys.shape, BF16),
             jax.ShapeDtypeStruct(values.shape, BF16),
+            jax.ShapeDtypeStruct((8, HD), F32),
         ),
         in_specs=[SMEM, wide, wide, narrow, narrow, front_spec, stats],
-        out_specs=(wide, narrow, narrow),
+        out_specs=(wide, narrow, narrow, pl.BlockSpec((8, HD), lambda k: (0, 0))),
         compiler_params=params(24),
         cost_estimate=cost(5, 384),
     )(length, query, grad, keys, values, front, full)
@@ -396,7 +399,7 @@
     return pl.pallas_call(
         functools.partial(add_kernel, num_prompts),
         out_shape=jax.ShapeDtypeStruct((copies, rows * num_prompts, HD), BF16),
-        in_specs=[VMEM, VMEM, pl.BlockSpec(memory_space=pl.ANY)],
+        in_specs=[VMEM, VMEM, VMEM],
         out_specs=VMEM,
         compiler_params=params(4),
     )(owners, terms, after)
@@ -459,11 +462,11 @@
     terms = exchange(
         front_grad.reshape(places * chips, rows, HD), ("prompt", "chip"), [FULL_ORDER]
     )
-    query_grad, key_grad, value_grad = rest_part(
+    query_grad, key_grad, value_grad, done = rest_part(
         lengths, query, grad, keys, values, front, full
     )
     terms = lax.all_gather(terms, "core", axis=0).reshape(-1, HD)
-    sums = add_by_prompt(owners, terms, key_grad, num_prompts, rows, chips)
+    sums = add_by_prompt(owners, terms, done, num_prompts, rows, chips)
     parts = exchange(sums, "chip", [NEAR_ORDER])
     prompt_key_grad, prompt_value_grad = place(parts, prompt_keys.shape)
     return (

time: 67.9 us -> 67.9 us (level)
    unnamed x18 -> x16, local copies, waits for them, and re-layouts: 3.12 us -> 3.12 us
where the time goes in v5:
time: 67.9 us; the launch traced here: 67.4 us
  starting transfers between devices  34.4 us (51%)
  blocking collectives  15.4 us (23%)
  Pallas kernels  12.8 us (19%)
  local copies, waits for them, and re-layouts  3.12 us (5%)
  between operations  1.39 us (2%)
    all_to_all x2, starting transfers between devices, exchange(): return lax.all_to_all(blocks, axes, 0, 0, axis_index_groups=groups)  34.4 us
    all_to_all x1, blocking collectives, exchange(): return lax.all_to_all(blocks, axes, 0, 0, axis_index_groups=groups)  11.7 us
    pallas_call x1, Pallas kernels, rest_part(): pl.pallas_call(rest_kernel, grid=(KVH,), out_shape=(jax.ShapeDtypeStruct(...  5.55 us
    all_gather x1, blocking collectives, shards(): terms = lax.all_gather(terms, 'core', axis=0).reshape(-1, HD)  3.67 us
    unnamed x16, local copies, waits for them, and re-layouts  3.12 us
    pallas_call x1, Pallas kernels, front_part(): pl.pallas_call(front_kernel, out_shape=(jax.ShapeDtypeStruct((shards_n, K...  2.53 us
    pallas_call x1, Pallas kernels, own_stats(): pl.pallas_call(own_kernel, out_shape=(jax.ShapeDtypeStruct((KVH, rows //...  2.03 us
    pallas_call x1, Pallas kernels, pick(): pl.pallas_call(pick_kernel, out_shape=jax.ShapeDtypeStruct((count, 2 * ro...  1.62 us
  transfers between devices with their start and end apart: 2, of which 1 were waited for; matrix products, arithmetic and copies ran while one was open for 0% of the time, Pallas kernels for 11%

profile of v5, /device:TPU:1, one launch (start us, length us, event | category | flops | bytes accessed | tf_op | source)
XLA Modules:
  0.0 67.4 jit_solution(196469352461256051)
XLA Ops:
  0.6 1.6 %shard_map.128 = bf16[16,16,512]{2,1,0:T(8,128)(2,1)} custom-call(s32[512]{0:T(512)} %group_hbm.1, bf16[8,8,512]{2,1,0:T(8,128)(2,1)} %keys_hbm.1, bf16[8,8,512]{2,1,0:T(8,128)(2,1)} %values_hbm.1), custom_call_target="tpu_custom_call" | custom-call | tf_op jit(solution)/shard_map/pallas_call | solution.py:138
  2.3 0.0 copy-start.4
  2.3 0.0 copy-start.5
  2.3 16.2 %all-to-all-start = ((bf16[16,16,512]{2,1,0:T(8,128)(2,1)}), bf16[16,16,512]{2,1,0:T(8,128)(2,1)S(1)}, u32[]{:S(2)}, u32[]{:S(2)}) async-start(bf16[16,16,512]{2,1,0:T(8,128)(2,1)} %shard_map.128), calls=%async_computation | async-start | bytes 524288 | tf_op jit(solution)/shard_map/all_to_all | solution.py:450
  18.5 0.0 copy-start.6
  19.1 0.0 copy-start.7
  19.2 0.0 copy-done.4
  19.2 0.0 copy-done.5
  19.2 0.0 copy-done.6
  19.2 0.6 copy-done.7
  19.8 0.0 copy-start
  19.8 1.2 %copy-done = bf16[1,256,2048]{2,1,0:T(8,128)(2,1)S(1)} copy-done((bf16[1,256,2048]{2,1,0:T(8,128)(2,1)S(1)}, bf16[1,256,2048]{2,1,0:T(8,128)(2,1)}, u32[]{:S(2)}) %copy-start) | copy-done | bytes 1048600
  21.1 0.0 copy-start.2
  21.1 1.2 %copy-done.2 = bf16[1,256,2048]{2,1,0:T(8,128)(2,1)S(1)} copy-done((bf16[1,256,2048]{2,1,0:T(8,128)(2,1)S(1)}, bf16[1,256,2048]{2,1,0:T(8,128)(2,1)}, u32[]{:S(2)}) %copy-start.2) | copy-done | bytes 1048600
  22.3 0.0 copy-start.1
  22.3 0.0 copy-start.3
  22.3 2.0 %shard_map.129 = (f32[4,2,8,512]{3,2,1,0:T(8,128)S(1)}, s32[1,2048]{1,0:T(1,128)S(1)}) custom-call(s32[1]{0:T(128)S(6)} %copy.14.length_ref, bf16[256,2048]{1,0:T(8,128)(2,1)S(1)} %bitcast.10, bf16[256,2048]{1,0:T(8,128)(2,1)S(1)} %bitcast.13, bf16[256,512]{1,0:T(8,128)(2,1)S(1)} %bitcast.17, bf16[256,512]{1,0:T(8,128)(2,1)S(1)} %bitcast.19, ...), custom_call_target="tpu_custom_call" | custom-call | flops 536870912 | bytes 3145728 | tf_op jit(solution)/shard_map/pallas_call | solution.py:336
  24.3 0.4 all-to-all-done.front_ref
  24.7 0.0 copy-done.1
  24.7 0.0 copy-done.3
  24.7 2.5 %shard_map.130 = (bf16[16,4,16,128]{3,2,1,0:T(8,128)(2,1)}, f32[4,2,8,512]{3,2,1,0:T(8,128)S(1)}) custom-call(s32[1]{0:T(128)S(6)} %copy.14.length_ref, bf16[256,2048]{1,0:T(8,128)(2,1)S(1)} %bitcast.11, bf16[256,2048]{1,0:T(8,128)(2,1)S(1)} %bitcast.14, bf16[16,16,512]{2,1,0:T(8,128)(2,1)S(1)} %all-to-all-done.front_ref, ...), custom_call_target="tpu_custom_call" | custom-call | flops 536870912 | bytes 3145728 | tf_op jit(solution)/shard_map/pallas_call | solution.py:351
  27.2 18.2 %all-to-all-start.1 = ((bf16[256,4,128]{2,1,0:T(4,128)(2,1)}), bf16[256,4,128]{2,1,0:T(4,128)(2,1)S(1)}, u32[]{:S(2)}, u32[]{:S(2)}) async-start(bf16[256,4,128]{2,1,0:T(4,128)(2,1)} %bitcast.8), calls=%async_computation.1 | async-start | bytes 524288 | tf_op jit(solution)/shard_map/all_to_all | solution.py:450
  45.4 5.6 %shard_map.131 = (bf16[256,2048]{1,0:T(8,128)(2,1)}, bf16[256,512]{1,0:T(8,128)(2,1)}, bf16[256,512]{1,0:T(8,128)(2,1)}, f32[8,128]{1,0:T(8,128)S(1)}) custom-call(s32[1]{0:T(128)S(6)} %copy.14.length_ref, bf16[256,2048]{1,0:T(8,128)(2,1)S(1)} %bitcast.12, bf16[256,2048]{1,0:T(8,128)(2,1)S(1)} %bitcast.15, bf16[256,512]{1,0:T(8,128)(2,1)S(1)} %bitcast.18, ...), custom_call_target="tpu_custom_call" | custom-call | flops 2013265920 | bytes 3145728 | tf_op jit(solution)/shard_map/pallas_call | solution.py:371
  51.0 0.0 all-to-all-done.1
  51.0 3.7 %all-gather = bf16[512,4,128]{2,1,0:T(4,128)(2,1)S(1)} all-gather(bf16[256,4,128]{2,1,0:T(4,128)(2,1)S(1)} %all-to-all-done.1), channel_id=2, replica_groups=mesh['prompt'=16,'chip'=16,'core'=2] {'core'}, dimensions={0}, use_global_device_ids=true | all-gather | bytes 786432 | tf_op jit(solution)/shard_map/all_gather | solution.py:468
  54.6 0.2 shard_map.132
  54.9 11.7 %all_to_all.15.parts_ref = bf16[16,32,128]{2,1,0:T(8,128)(2,1)S(1)} all-to-all(bf16[16,32,128]{2,1,0:T(8,128)(2,1)S(1)} %shard_map.132), channel_id=1, replica_groups={{8,10,12,14,0,2,4,6,24,26,28,30,16,18,20,22},{9,11,13,15,1,3,5,7,25,27,..., dimensions={0} | all-to-all | bytes 262144 | tf_op jit(solution)/shard_map/all_to_all | solution.py:450
  66.6 0.9 %shard_map.133 = (f32[8,8,512]{2,1,0:T(8,128)}, f32[8,8,512]{2,1,0:T(8,128)}) custom-call(bf16[16,32,128]{2,1,0:T(8,128)(2,1)S(1)} %all_to_all.15.parts_ref), custom_call_target="tpu_custom_call" | custom-call | tf_op jit(solution)/shard_map/pallas_call | solution.py:436
Async XLA Ops:
  2.3 16.9 %copy-start.4 = (bf16[1,256,512]{2,1,0:T(8,128)(2,1)S(1)}, bf16[1,256,512]{2,1,0:T(8,128)(2,1)}, u32[]{:S(2)}) copy-start(bf16[1,256,512]{2,1,0:T(8,128)(2,1)} %param.10) | copy-start | bytes 786436
  2.3 16.9 %copy-start.5 = (bf16[1,256,512]{2,1,0:T(8,128)(2,1)S(1)}, bf16[1,256,512]{2,1,0:T(8,128)(2,1)}, u32[]{:S(2)}) copy-start(bf16[1,256,512]{2,1,0:T(8,128)(2,1)} %param.11) | copy-start | bytes 786436
  2.3 22.4 %all-to-all-start = ((bf16[16,16,512]{2,1,0:T(8,128)(2,1)}), bf16[16,16,512]{2,1,0:T(8,128)(2,1)S(1)}, u32[]{:S(2)}, u32[]{:S(2)}) async-start(bf16[16,16,512]{2,1,0:T(8,128)(2,1)} %shard_map.128), calls=%async_computation | async-start | bytes 524288 | tf_op jit(solution)/shard_map/all_to_all | solution.py:450
  18.5 0.7 %copy-start.6 = (s32[1,2048]{1,0:T(1,128)S(1)}, s32[1,2048]{1,0:T(1,128)}, u32[]{:S(2)}) copy-start(s32[1,2048]{1,0:T(1,128)} %constant.2.clone.slots_ref) | copy-start | bytes 24580
  19.1 0.7 %copy-start.7 = (s32[512]{0:T(512)S(1)}, s32[512]{0:T(512)}, u32[]{:S(2)}) copy-start(s32[512]{0:T(512)} %group_hbm.1) | copy-start | bytes 6148
  19.8 1.2 %copy-start = (bf16[1,256,2048]{2,1,0:T(8,128)(2,1)S(1)}, bf16[1,256,2048]{2,1,0:T(8,128)(2,1)}, u32[]{:S(2)}) copy-start(bf16[1,256,2048]{2,1,0:T(8,128)(2,1)} %param.9) | copy-start | bytes 3145732
  21.1 1.2 %copy-start.2 = (bf16[1,256,2048]{2,1,0:T(8,128)(2,1)S(1)}, bf16[1,256,2048]{2,1,0:T(8,128)(2,1)}, u32[]{:S(2)}) copy-start(bf16[1,256,2048]{2,1,0:T(8,128)(2,1)} %param.14) | copy-start | bytes 3145732
  22.3 2.4 %copy-start.1 = (bf16[1,256,2048]{2,1,0:T(8,128)(2,1)S(1)}, bf16[1,256,2048]{2,1,0:T(8,128)(2,1)}, u32[]{:S(2)}) copy-start(bf16[1,256,2048]{2,1,0:T(8,128)(2,1)} %param.9) | copy-start | bytes 3145732
  22.3 2.4 %copy-start.3 = (bf16[1,256,2048]{2,1,0:T(8,128)(2,1)S(1)}, bf16[1,256,2048]{2,1,0:T(8,128)(2,1)}, u32[]{:S(2)}) copy-start(bf16[1,256,2048]{2,1,0:T(8,128)(2,1)} %param.14) | copy-start | bytes 3145732
  27.2 23.7 %all-to-all-start.1 = ((bf16[256,4,128]{2,1,0:T(4,128)(2,1)}), bf16[256,4,128]{2,1,0:T(4,128)(2,1)S(1)}, u32[]{:S(2)}, u32[]{:S(2)}) async-start(bf16[256,4,128]{2,1,0:T(4,128)(2,1)} %bitcast.8), calls=%async_computation.1 | async-start | bytes 524288 | tf_op jit(solution)/shard_map/all_to_all | solution.py:450

commit v6 on v5

--- a/solution.py
+++ b/solution.py
@@ -43,9 +43,9 @@
 
 
 PLACE_ORDER = far_first(PLACES, (1, 2), LATE_PLACE)
-CHIP_ORDER = far_first(CHIPS, (1, 1), LATE_CHIP)
-NEAR_ORDER = [c ^ CHIP_ORDER[0] for c in range(len(CHIP_ORDER))]
-FULL_ORDER = [p * len(CHIP_ORDER) + c for p in PLACE_ORDER for c in CHIP_ORDER]
+ROW_ORDER = far_first((1, CHIPS[1]), (1, 1), (0, LATE_CHIP[1]))
+NEAR_ORDER = [row ^ LATE_CHIP[1] for row in range(CHIPS[1])]
+CHIP_COUNT = CHIPS[0] * CHIPS[1]
 
 
 def nt_dot(a, b):
@@ -99,9 +99,25 @@
     return (1 - side if bent else side) * CHIPS[1] + row
 
 
+def sum_groups():
+    return [
+        [
+            place * CHIP_COUNT + peer_chip(side, row, place)
+            for place in PLACE_ORDER
+            for row in ROW_ORDER
+        ]
+        for side in range(CHIPS[0])
+    ]
+
+
+def own_side(chip):
+    bent = lax.axis_index("prompt") % PLACES[1] >= PLACES[1] // 2
+    return jnp.where(bent, 1 - chip // CHIPS[1], chip // CHIPS[1])
+
+
 def front_groups():
     return [
-        [place * len(CHIP_ORDER) + peer_chip(side, row, place) for place in PLACE_ORDER]
+        [place * CHIP_COUNT + peer_chip(side, row, place) for place in PLACE_ORDER]
         for side in range(CHIPS[0])
         for row in range(CHIPS[1])
     ]
@@ -120,12 +136,11 @@
         copy.start()
     chip, core = lax.axis_index("chip"), lax.axis_index("core")
     row = chip % CHIPS[1]
-    bent = lax.axis_index("prompt") % PLACES[1] >= PLACES[1] // 2
-    side = jnp.where(bent, 1 - chip // CHIPS[1], chip // CHIPS[1])
+    side = own_side(chip)
     for copy in copies:
         copy.wait()
     for i, place in enumerate(PLACE_ORDER):
-        peer = place * len(CHIP_ORDER) + peer_chip(side, row, place)
+        peer = place * CHIP_COUNT + peer_chip(side, row, place)
         owner = group_ref[peer * CORES + core]
         both = jnp.concatenate(
             [keys_ref[owner].astype(F32), values_ref[owner].astype(F32)], axis=0
@@ -177,7 +192,10 @@
             fill = jnp.zeros((5, top.shape[1]), F32)
             stats_ref[k, half] = jnp.concatenate([top, total, dot, fill], axis=0)
     count, size = group_ref.shape[1], slots_ref.shape[1]
-    hit = lax.broadcasted_iota(jnp.int32, (count, size), 0) == slots_ref[...]
+    side = own_side(lax.axis_index("chip"))
+    slots = jnp.where(side == 0, slots_ref[0:1], slots_ref[1:2])
+    slots = slots + lax.axis_index("core")
+    hit = lax.broadcasted_iota(jnp.int32, (count, size), 0) == slots
     group = jnp.broadcast_to(group_ref[...].astype(F32).astype(BF16), (8, count))
     owners = nn_dot(group, jnp.where(hit, 1.0, 0.0).astype(BF16))
     owners_ref[...] = owners[:1].astype(jnp.int32)
@@ -331,13 +349,12 @@
 
 def own_stats(length, query, grad, keys, values, group, copies):
     rows = query.shape[0]
-    slots = [m * CORES + core for core in range(CORES) for m in FULL_ORDER]
-    slots = np.repeat(np.array(slots, np.int32), copies)[None]
+    slots = np.repeat(np.array(sum_groups(), np.int32) * CORES, copies, axis=1)
     return pl.pallas_call(
         own_kernel,
         out_shape=(
             jax.ShapeDtypeStruct((KVH, rows // HALF, 8, GROUP * HALF), F32),
-            jax.ShapeDtypeStruct(slots.shape, jnp.int32),
+            jax.ShapeDtypeStruct((1, slots.shape[1]), jnp.int32),
         ),
         in_specs=[SMEM] + [VMEM] * 6,
         out_specs=(VMEM, VMEM),
@@ -386,46 +403,48 @@
 
 def add_kernel(num_prompts, owners_ref, terms_ref, _, out_ref):
     count = terms_ref.shape[0]
-    total = out_ref.shape[1]
+    total = out_ref.shape[0]
     rows = total // num_prompts
     row_ids = lax.broadcasted_iota(jnp.int32, (total, count), 0)
     col_ids = lax.broadcasted_iota(jnp.int32, (total, count), 1)
     hit = (owners_ref[...] == row_ids // rows) & (row_ids % rows == col_ids % rows)
-    sums = nn_dot(jnp.where(hit, 1.0, 0.0).astype(BF16), terms_ref[...]).astype(BF16)
-    out_ref[...] = jnp.broadcast_to(sums[None], out_ref.shape)
-
-
-def add_by_prompt(owners, terms, after, num_prompts, rows, copies):
+    hit = jnp.where(hit, 1.0, 0.0).astype(BF16)
+    out_ref[...] = nn_dot(hit, terms_ref[...]).astype(BF16)
+
+
+def add_by_prompt(owners, terms, after, num_prompts, rows):
     return pl.pallas_call(
         functools.partial(add_kernel, num_prompts),
-        out_shape=jax.ShapeDtypeStruct((copies, rows * num_prompts, HD), BF16),
+        out_shape=jax.ShapeDtypeStruct((rows * num_prompts, HD), BF16),
         in_specs=[VMEM, VMEM, VMEM],
         out_specs=VMEM,
         compiler_params=params(4),
     )(owners, terms, after)
 
 
+def spread_kernel(sums_ref, out_ref):
+    total = jnp.sum(sums_ref[...].astype(F32), axis=0).astype(BF16)
+    out_ref[...] = jnp.broadcast_to(total[None], out_ref.shape)
+
+
+def spread(sums, copies):
+    return pl.pallas_call(
+        spread_kernel,
+        out_shape=jax.ShapeDtypeStruct((copies,) + sums.shape[1:], BF16),
+        in_specs=[VMEM],
+        out_specs=VMEM,
+        compiler_params=params(4),
+    )(sums)
+
+
 def place_kernel(parts_ref, key_hbm, value_hbm, out_ref, sems):
-    came = [NEAR_ORDER.index(chip) for chip in CHIP_ORDER]
     _, prompts, own, _ = out_ref.shape
-    blocks = parts_ref.shape[0] // (2 * KVH)
-    rows = own // blocks
-    size = prompts * own
-    to = lax.broadcasted_iota(jnp.int32, (size, size), 0)
-    at = lax.broadcasted_iota(jnp.int32, (size, size), 1)
-    prompt, row = to // own, to % own
-    hit = at == (row // rows) * (rows * prompts) + prompt * rows + row % rows
-    move = jnp.where(hit, 1.0, 0.0).astype(BF16)
+    came = [NEAR_ORDER.index(row) for row in ROW_ORDER]
     copies = []
     for side, out_hbm in enumerate((key_hbm, value_hbm)):
         for k in range(KVH):
-            first = (k * 2 + side) * blocks
-            block = jnp.concatenate(
-                [parts_ref[came[first + w]] for w in range(blocks)], axis=0
-            )
-            out_ref[side, :, :, k * HD : (k + 1) * HD] = nn_dot(move, block).reshape(
-                prompts, own, HD
-            )
+            block = parts_ref[came[k * 2 + side]].astype(F32)
+            out_ref[side, :, :, k * HD : (k + 1) * HD] = block.reshape(prompts, own, HD)
         copies.append(pltpu.make_async_copy(out_ref.at[side], out_hbm, sems.at[side]))
         copies[-1].start()
     for copy in copies:
@@ -451,23 +470,28 @@
 
 
 def shards(query, resp_keys, resp_values, prompt_keys, prompt_values, out_grad, group, lengths):
-    places, chips = lax.axis_size("prompt"), lax.axis_size("chip")
-    num_prompts, own, width = prompt_keys.shape
+    places = lax.axis_size("prompt")
+    num_prompts, own, _ = prompt_keys.shape
     wanted = pick(group, prompt_keys, prompt_values, places)
     front = exchange(wanted, ("prompt", "chip"), front_groups())
     query, grad, keys, values = query[0], out_grad[0], resp_keys[0], resp_values[0]
-    rows = 2 * own * width // (chips * HD)
+    rows = own
     stats, owners = own_stats(lengths, query, grad, keys, values, group, rows)
     front_grad, full = front_part(lengths, query, grad, front, stats)
     terms = exchange(
-        front_grad.reshape(places * chips, rows, HD), ("prompt", "chip"), [FULL_ORDER]
+        front_grad.reshape(-1, rows, HD), ("prompt", "chip"), sum_groups()
     )
     query_grad, key_grad, value_grad, done = rest_part(
         lengths, query, grad, keys, values, front, full
     )
-    terms = lax.all_gather(terms, "core", axis=0).reshape(-1, HD)
-    sums = add_by_prompt(owners, terms, done, num_prompts, rows, chips)
-    parts = exchange(sums, "chip", [NEAR_ORDER])
+    sums = add_by_prompt(owners, terms.reshape(-1, HD), done, num_prompts, rows)
+    near = [
+        [(z * CHIPS[1] + row) * CORES + core for z in range(CHIPS[0]) for core in range(CORES)]
+        for row in range(CHIPS[1])
+    ]
+    sums = lax.all_gather(sums, ("chip", "core"), axis=0, axis_index_groups=near)
+    along = [[z * CHIPS[1] + row for row in NEAR_ORDER] for z in range(CHIPS[0])]
+    parts = exchange(spread(sums, CHIPS[1]), "chip", along)
     prompt_key_grad, prompt_value_grad = place(parts, prompt_keys.shape)
     return (
         query_grad[None],

time: 67.9 us -> 70.4 us (1.037)
  blocking collectives: 15.4 us -> 18.4 us
    all_gather x1, blocking collectives: 3.67 us -> 7.15 us  [shards(): lax.all_gather(sums, ('chip', 'core'), axis=0, axis_index_groups=near)]
  transfers between devices with their start and end apart: 2 -> 2, of which waited for: 1 -> 2; matrix products, arithmetic and copies ran while one was open for 0% -> 0% of each run, Pallas kernels for 11% -> 11%
where the time goes in v6:
time: 70.4 us; the launch traced here: 69.9 us
  starting transfers between devices  33.7 us (48%)
  blocking collectives  18.4 us (26%)
  Pallas kernels  12.5 us (18%)
  local copies, waits for them, and re-layouts  3.12 us (4%)
  between operations  1.39 us (2%)
  waiting for transfers between devices  0.84 us (1%)
    all_to_all x2, starting transfers between devices, exchange(): return lax.all_to_all(blocks, axes, 0, 0, axis_index_groups=groups)  33.7 us
    all_to_all x1, blocking collectives, exchange(): return lax.all_to_all(blocks, axes, 0, 0, axis_index_groups=groups)  11.2 us
    all_gather x1, blocking collectives, shards(): lax.all_gather(sums, ('chip', 'core'), axis=0, axis_index_groups=near)  7.15 us
    pallas_call x1, Pallas kernels, rest_part(): pl.pallas_call(rest_kernel, grid=(KVH,), out_shape=(jax.ShapeDtypeStruct(...  5.57 us
    unnamed x16, local copies, waits for them, and re-layouts  3.12 us
    pallas_call x1, Pallas kernels, front_part(): pl.pallas_call(front_kernel, out_shape=(jax.ShapeDtypeStruct((shards_n, K...  2.55 us
    pallas_call x1, Pallas kernels, own_stats(): pl.pallas_call(own_kernel, out_shape=(jax.ShapeDtypeStruct((KVH, rows //...  1.85 us
    pallas_call x1, Pallas kernels, pick(): pl.pallas_call(pick_kernel, out_shape=jax.ShapeDtypeStruct((count, 2 * ro...  1.62 us
  transfers between devices with their start and end apart: 2, of which 2 were waited for; matrix products, arithmetic and copies ran while one was open for 0% of the time, Pallas kernels for 11%

profile of v6, /device:TPU:1, one launch (start us, length us, event | category | flops | bytes accessed | tf_op | source)
XLA Modules:
  0.0 69.9 jit_solution(4977388694090374835)
XLA Ops:
  0.6 1.6 %shard_map.128 = bf16[16,16,512]{2,1,0:T(8,128)(2,1)} custom-call(s32[512]{0:T(512)} %group_hbm.1, bf16[8,8,512]{2,1,0:T(8,128)(2,1)} %keys_hbm.1, bf16[8,8,512]{2,1,0:T(8,128)(2,1)} %values_hbm.1), custom_call_target="tpu_custom_call" | custom-call | tf_op jit(solution)/shard_map/pallas_call | solution.py:153
  2.3 0.0 copy-start.4
  2.3 0.0 copy-start.5
  2.3 16.2 %all-to-all-start = ((bf16[16,16,512]{2,1,0:T(8,128)(2,1)}), bf16[16,16,512]{2,1,0:T(8,128)(2,1)S(1)}, u32[]{:S(2)}, u32[]{:S(2)}) async-start(bf16[16,16,512]{2,1,0:T(8,128)(2,1)} %shard_map.128), calls=%async_computation | async-start | bytes 524288 | tf_op jit(solution)/shard_map/all_to_all | solution.py:469
  18.5 0.0 copy-start.6
  19.1 0.0 copy-start.7
  19.2 0.0 copy-done.4
  19.2 0.0 copy-done.5
  19.2 0.0 copy-done.6
  19.2 0.6 copy-done.7
  19.8 0.0 copy-start
  19.8 1.2 %copy-done = bf16[1,256,2048]{2,1,0:T(8,128)(2,1)S(1)} copy-done((bf16[1,256,2048]{2,1,0:T(8,128)(2,1)S(1)}, bf16[1,256,2048]{2,1,0:T(8,128)(2,1)}, u32[]{:S(2)}) %copy-start) | copy-done | bytes 1048600
  21.1 0.0 copy-start.2
  21.1 1.2 %copy-done.2 = bf16[1,256,2048]{2,1,0:T(8,128)(2,1)S(1)} copy-done((bf16[1,256,2048]{2,1,0:T(8,128)(2,1)S(1)}, bf16[1,256,2048]{2,1,0:T(8,128)(2,1)}, u32[]{:S(2)}) %copy-start.2) | copy-done | bytes 1048600
  22.3 0.0 copy-start.1
  22.3 0.0 copy-start.3
  22.3 1.9 %shard_map.129 = (f32[4,2,8,512]{3,2,1,0:T(8,128)S(1)}, s32[1,1024]{1,0:T(1,128)S(1)}) custom-call(s32[1]{0:T(128)S(6)} %copy.14.length_ref, bf16[256,2048]{1,0:T(8,128)(2,1)S(1)} %bitcast.11, bf16[256,2048]{1,0:T(8,128)(2,1)S(1)} %bitcast.14, bf16[256,512]{1,0:T(8,128)(2,1)S(1)} %bitcast.18, bf16[256,512]{1,0:T(8,128)(2,1)S(1)} %bitcast.20, ...), custom_call_target="tpu_custom_call" | custom-call | flops 536870912 | bytes 3145728 | tf_op jit(solution)/shard_map/pallas_call | solution.py:353
  24.1 0.5 all-to-all-done.front_ref
  24.7 0.0 copy-done.1
  24.7 0.0 copy-done.3
  24.7 2.6 %shard_map.130 = (bf16[16,4,16,128]{3,2,1,0:T(8,128)(2,1)}, f32[4,2,8,512]{3,2,1,0:T(8,128)S(1)}) custom-call(s32[1]{0:T(128)S(6)} %copy.14.length_ref, bf16[256,2048]{1,0:T(8,128)(2,1)S(1)} %bitcast.12, bf16[256,2048]{1,0:T(8,128)(2,1)S(1)} %bitcast.15, bf16[16,16,512]{2,1,0:T(8,128)(2,1)S(1)} %all-to-all-done.front_ref, ...), custom_call_target="tpu_custom_call" | custom-call | flops 536870912 | bytes 3145728 | tf_op jit(solution)/shard_map/pallas_call | solution.py:368
  27.3 17.5 %all-to-all-start.1 = ((bf16[128,8,128]{2,1,0:T(8,128)(2,1)}), bf16[128,8,128]{2,1,0:T(8,128)(2,1)S(1)}, u32[]{:S(2)}, u32[]{:S(2)}) async-start(bf16[128,8,128]{2,1,0:T(8,128)(2,1)} %bitcast.8), calls=%async_computation.1 | async-start | bytes 524288 | tf_op jit(solution)/shard_map/all_to_all | solution.py:469
  44.7 5.6 %shard_map.131 = (bf16[256,2048]{1,0:T(8,128)(2,1)}, bf16[256,512]{1,0:T(8,128)(2,1)}, bf16[256,512]{1,0:T(8,128)(2,1)}, f32[8,128]{1,0:T(8,128)S(1)}) custom-call(s32[1]{0:T(128)S(6)} %copy.14.length_ref, bf16[256,2048]{1,0:T(8,128)(2,1)S(1)} %bitcast.13, bf16[256,2048]{1,0:T(8,128)(2,1)S(1)} %bitcast.16, bf16[256,512]{1,0:T(8,128)(2,1)S(1)} %bitcast.19, ...), custom_call_target="tpu_custom_call" | custom-call | flops 2013265920 | bytes 3145728 | tf_op jit(solution)/shard_map/pallas_call | solution.py:388
  50.3 0.3 all-to-all-done.1
  50.6 0.2 shard_map.132
  50.8 7.1 %all-gather = bf16[256,128]{1,0:T(8,128)(2,1)S(1)} all-gather(bf16[64,128]{1,0:T(8,128)(2,1)S(1)} %shard_map.132), channel_id=2, replica_groups={{0,1,16,17},{2,3,18,19},{4,5,20,21},{6,7,22,23},{8,9,24,25},{10,11,26,2..., dimensions={0}, use_global_device_ids=true | all-gather | bytes 81920 | tf_op jit(solution)/shard_map/all_gather | solution.py:492
  57.9 11.2 %all_to_all.15.parts_ref = bf16[8,64,128]{2,1,0:T(8,128)(2,1)S(1)} all-to-all(bf16[8,64,128]{2,1,0:T(8,128)(2,1)S(1)} %shard_map.133), channel_id=1, replica_groups={{8,10,12,14,0,2,4,6},{24,26,28,30,16,18,20,22},{9,11,13,15,1,3,5,7},{25..., dimensions={0} | all-to-all | bytes 262144 | tf_op jit(solution)/shard_map/all_to_all | solution.py:469
  69.2 0.7 %shard_map.134 = (f32[8,8,512]{2,1,0:T(8,128)}, f32[8,8,512]{2,1,0:T(8,128)}) custom-call(bf16[8,64,128]{2,1,0:T(8,128)(2,1)S(1)} %all_to_all.15.parts_ref), custom_call_target="tpu_custom_call" | custom-call | tf_op jit(solution)/shard_map/pallas_call | solution.py:455
  (1 shorter events, 0.0 us)
Async XLA Ops:
  2.3 16.9 %copy-start.4 = (bf16[1,256,512]{2,1,0:T(8,128)(2,1)S(1)}, bf16[1,256,512]{2,1,0:T(8,128)(2,1)}, u32[]{:S(2)}) copy-start(bf16[1,256,512]{2,1,0:T(8,128)(2,1)} %param.10) | copy-start | bytes 786436
  2.3 16.9 %copy-start.5 = (bf16[1,256,512]{2,1,0:T(8,128)(2,1)S(1)}, bf16[1,256,512]{2,1,0:T(8,128)(2,1)}, u32[]{:S(2)}) copy-start(bf16[1,256,512]{2,1,0:T(8,128)(2,1)} %param.11) | copy-start | bytes 786436
  2.3 22.4 %all-to-all-start = ((bf16[16,16,512]{2,1,0:T(8,128)(2,1)}), bf16[16,16,512]{2,1,0:T(8,128)(2,1)S(1)}, u32[]{:S(2)}, u32[]{:S(2)}) async-start(bf16[16,16,512]{2,1,0:T(8,128)(2,1)} %shard_map.128), calls=%async_computation | async-start | bytes 524288 | tf_op jit(solution)/shard_map/all_to_all | solution.py:469
  18.5 0.7 %copy-start.6 = (s32[2,1024]{1,0:T(2,128)S(1)}, s32[2,1024]{1,0:T(2,128)}, u32[]{:S(2)}) copy-start(s32[2,1024]{1,0:T(2,128)} %constant.2.clone.slots_ref) | copy-start | bytes 24580
  19.1 0.7 copy-start.7
  19.8 1.2 %copy-start = (bf16[1,256,2048]{2,1,0:T(8,128)(2,1)S(1)}, bf16[1,256,2048]{2,1,0:T(8,128)(2,1)}, u32[]{:S(2)}) copy-start(bf16[1,256,2048]{2,1,0:T(8,128)(2,1)} %param.9) | copy-start | bytes 3145732
  21.1 1.2 %copy-start.2 = (bf16[1,256,2048]{2,1,0:T(8,128)(2,1)S(1)}, bf16[1,256,2048]{2,1,0:T(8,128)(2,1)}, u32[]{:S(2)}) copy-start(bf16[1,256,2048]{2,1,0:T(8,128)(2,1)} %param.14) | copy-start | bytes 3145732
  22.3 2.4 %copy-start.1 = (bf16[1,256,2048]{2,1,0:T(8,128)(2,1)S(1)}, bf16[1,256,2048]{2,1,0:T(8,128)(2,1)}, u32[]{:S(2)}) copy-start(bf16[1,256,2048]{2,1,0:T(8,128)(2,1)} %param.9) | copy-start | bytes 3145732
  22.3 2.4 %copy-start.3 = (bf16[1,256,2048]{2,1,0:T(8,128)(2,1)S(1)}, bf16[1,256,2048]{2,1,0:T(8,128)(2,1)}, u32[]{:S(2)}) copy-start(bf16[1,256,2048]{2,1,0:T(8,128)(2,1)} %param.14) | copy-start | bytes 3145732
  27.3 23.3 %all-to-all-start.1 = ((bf16[128,8,128]{2,1,0:T(8,128)(2,1)}), bf16[128,8,128]{2,1,0:T(8,128)(2,1)S(1)}, u32[]{:S(2)}, u32[]{:S(2)}) async-start(bf16[128,8,128]{2,1,0:T(8,128)(2,1)} %bitcast.8), calls=%async_computation.1 | async-start | bytes 524288 | tf_op jit(solution)/shard_map/all_to_all | solution.py:469

commit v7 on v5

--- a/solution.py
+++ b/solution.py
@@ -410,21 +410,16 @@
     _, prompts, own, _ = out_ref.shape
     blocks = parts_ref.shape[0] // (2 * KVH)
     rows = own // blocks
-    size = prompts * own
-    to = lax.broadcasted_iota(jnp.int32, (size, size), 0)
-    at = lax.broadcasted_iota(jnp.int32, (size, size), 1)
-    prompt, row = to // own, to % own
-    hit = at == (row // rows) * (rows * prompts) + prompt * rows + row % rows
-    move = jnp.where(hit, 1.0, 0.0).astype(BF16)
     copies = []
     for side, out_hbm in enumerate((key_hbm, value_hbm)):
         for k in range(KVH):
             first = (k * 2 + side) * blocks
-            block = jnp.concatenate(
-                [parts_ref[came[first + w]] for w in range(blocks)], axis=0
-            )
-            out_ref[side, :, :, k * HD : (k + 1) * HD] = nn_dot(move, block).reshape(
-                prompts, own, HD
+            out_ref[side, :, :, k * HD : (k + 1) * HD] = jnp.concatenate(
+                [
+                    parts_ref[came[first + w]].astype(F32).reshape(prompts, rows, HD)
+                    for w in range(blocks)
+                ],
+                axis=1,
             )
         copies.append(pltpu.make_async_copy(out_ref.at[side], out_hbm, sems.at[side]))
         copies[-1].start()

time: 67.9 us -> 67.8 us (level)
  no operation moved by 1% of the time
where the time goes in v7:
time: 67.8 us; the launch traced here: 67.3 us
  starting transfers between devices  34.4 us (51%)
  blocking collectives  15.4 us (23%)
  Pallas kernels  12.7 us (19%)
  local copies, waits for them, and re-layouts  3.12 us (5%)
  between operations  1.39 us (2%)
    all_to_all x2, starting transfers between devices, exchange(): return lax.all_to_all(blocks, axes, 0, 0, axis_index_groups=groups)  34.4 us
    all_to_all x1, blocking collectives, exchange(): return lax.all_to_all(blocks, axes, 0, 0, axis_index_groups=groups)  11.7 us
    pallas_call x1, Pallas kernels, rest_part(): pl.pallas_call(rest_kernel, grid=(KVH,), out_shape=(jax.ShapeDtypeStruct(...  5.55 us
    all_gather x1, blocking collectives, shards(): terms = lax.all_gather(terms, 'core', axis=0).reshape(-1, HD)  3.67 us
    unnamed x16, local copies, waits for them, and re-layouts  3.12 us
    pallas_call x1, Pallas kernels, front_part(): pl.pallas_call(front_kernel, out_shape=(jax.ShapeDtypeStruct((shards_n, K...  2.53 us
    pallas_call x1, Pallas kernels, own_stats(): pl.pallas_call(own_kernel, out_shape=(jax.ShapeDtypeStruct((KVH, rows //...  2.03 us
    pallas_call x1, Pallas kernels, pick(): pl.pallas_call(pick_kernel, out_shape=jax.ShapeDtypeStruct((count, 2 * ro...  1.62 us
  transfers between devices with their start and end apart: 2, of which 1 were waited for; matrix products, arithmetic and copies ran while one was open for 0% of the time, Pallas kernels for 11%

profile of v7, /device:TPU:1, one launch (start us, length us, event | category | flops | bytes accessed | tf_op | source)
XLA Modules:
  0.0 67.3 jit_solution(10095618364244903239)
XLA Ops:
  0.6 1.6 %shard_map.128 = bf16[16,16,512]{2,1,0:T(8,128)(2,1)} custom-call(s32[512]{0:T(512)} %group_hbm.1, bf16[8,8,512]{2,1,0:T(8,128)(2,1)} %keys_hbm.1, bf16[8,8,512]{2,1,0:T(8,128)(2,1)} %values_hbm.1), custom_call_target="tpu_custom_call" | custom-call | tf_op jit(solution)/shard_map/pallas_call | solution.py:138
  2.3 0.0 copy-start.4
  2.3 0.0 copy-start.5
  2.3 16.2 %all-to-all-start = ((bf16[16,16,512]{2,1,0:T(8,128)(2,1)}), bf16[16,16,512]{2,1,0:T(8,128)(2,1)S(1)}, u32[]{:S(2)}, u32[]{:S(2)}) async-start(bf16[16,16,512]{2,1,0:T(8,128)(2,1)} %shard_map.128), calls=%async_computation | async-start | bytes 524288 | tf_op jit(solution)/shard_map/all_to_all | solution.py:445
  18.5 0.0 copy-start.6
  19.1 0.0 copy-start.7
  19.2 0.0 copy-done.4
  19.2 0.0 copy-done.5
  19.2 0.0 copy-done.6
  19.2 0.6 copy-done.7
  19.8 0.0 copy-start
  19.8 1.2 %copy-done = bf16[1,256,2048]{2,1,0:T(8,128)(2,1)S(1)} copy-done((bf16[1,256,2048]{2,1,0:T(8,128)(2,1)S(1)}, bf16[1,256,2048]{2,1,0:T(8,128)(2,1)}, u32[]{:S(2)}) %copy-start) | copy-done | bytes 1048600
  21.1 0.0 copy-start.2
  21.1 1.2 %copy-done.2 = bf16[1,256,2048]{2,1,0:T(8,128)(2,1)S(1)} copy-done((bf16[1,256,2048]{2,1,0:T(8,128)(2,1)S(1)}, bf16[1,256,2048]{2,1,0:T(8,128)(2,1)}, u32[]{:S(2)}) %copy-start.2) | copy-done | bytes 1048600
  22.3 0.0 copy-start.1
  22.3 0.0 copy-start.3
  22.3 2.0 %shard_map.129 = (f32[4,2,8,512]{3,2,1,0:T(8,128)S(1)}, s32[1,2048]{1,0:T(1,128)S(1)}) custom-call(s32[1]{0:T(128)S(6)} %copy.14.length_ref, bf16[256,2048]{1,0:T(8,128)(2,1)S(1)} %bitcast.10, bf16[256,2048]{1,0:T(8,128)(2,1)S(1)} %bitcast.13, bf16[256,512]{1,0:T(8,128)(2,1)S(1)} %bitcast.17, bf16[256,512]{1,0:T(8,128)(2,1)S(1)} %bitcast.19, ...), custom_call_target="tpu_custom_call" | custom-call | flops 536870912 | bytes 3145728 | tf_op jit(solution)/shard_map/pallas_call | solution.py:336
  24.3 0.4 all-to-all-done.front_ref
  24.7 0.0 copy-done.1
  24.7 0.0 copy-done.3
  24.7 2.5 %shard_map.130 = (bf16[16,4,16,128]{3,2,1,0:T(8,128)(2,1)}, f32[4,2,8,512]{3,2,1,0:T(8,128)S(1)}) custom-call(s32[1]{0:T(128)S(6)} %copy.14.length_ref, bf16[256,2048]{1,0:T(8,128)(2,1)S(1)} %bitcast.11, bf16[256,2048]{1,0:T(8,128)(2,1)S(1)} %bitcast.14, bf16[16,16,512]{2,1,0:T(8,128)(2,1)S(1)} %all-to-all-done.front_ref, ...), custom_call_target="tpu_custom_call" | custom-call | flops 536870912 | bytes 3145728 | tf_op jit(solution)/shard_map/pallas_call | solution.py:351
  27.2 18.2 %all-to-all-start.1 = ((bf16[256,4,128]{2,1,0:T(4,128)(2,1)}), bf16[256,4,128]{2,1,0:T(4,128)(2,1)S(1)}, u32[]{:S(2)}, u32[]{:S(2)}) async-start(bf16[256,4,128]{2,1,0:T(4,128)(2,1)} %bitcast.8), calls=%async_computation.1 | async-start | bytes 524288 | tf_op jit(solution)/shard_map/all_to_all | solution.py:445
  45.4 5.6 %shard_map.131 = (bf16[256,2048]{1,0:T(8,128)(2,1)}, bf16[256,512]{1,0:T(8,128)(2,1)}, bf16[256,512]{1,0:T(8,128)(2,1)}, f32[8,128]{1,0:T(8,128)S(1)}) custom-call(s32[1]{0:T(128)S(6)} %copy.14.length_ref, bf16[256,2048]{1,0:T(8,128)(2,1)S(1)} %bitcast.12, bf16[256,2048]{1,0:T(8,128)(2,1)S(1)} %bitcast.15, bf16[256,512]{1,0:T(8,128)(2,1)S(1)} %bitcast.18, ...), custom_call_target="tpu_custom_call" | custom-call | flops 2013265920 | bytes 3145728 | tf_op jit(solution)/shard_map/pallas_call | solution.py:371
  51.0 0.0 all-to-all-done.1
  51.0 3.7 %all-gather = bf16[512,4,128]{2,1,0:T(4,128)(2,1)S(1)} all-gather(bf16[256,4,128]{2,1,0:T(4,128)(2,1)S(1)} %all-to-all-done.1), channel_id=2, replica_groups=mesh['prompt'=16,'chip'=16,'core'=2] {'core'}, dimensions={0}, use_global_device_ids=true | all-gather | bytes 786432 | tf_op jit(solution)/shard_map/all_gather | solution.py:463
  54.6 0.2 shard_map.132
  54.9 11.7 %all_to_all.15.parts_ref = bf16[16,32,128]{2,1,0:T(8,128)(2,1)S(1)} all-to-all(bf16[16,32,128]{2,1,0:T(8,128)(2,1)S(1)} %shard_map.132), channel_id=1, replica_groups={{8,10,12,14,0,2,4,6,24,26,28,30,16,18,20,22},{9,11,13,15,1,3,5,7,25,27,..., dimensions={0} | all-to-all | bytes 262144 | tf_op jit(solution)/shard_map/all_to_all | solution.py:445
  66.6 0.7 %shard_map.133 = (f32[8,8,512]{2,1,0:T(8,128)}, f32[8,8,512]{2,1,0:T(8,128)}) custom-call(bf16[16,32,128]{2,1,0:T(8,128)(2,1)S(1)} %all_to_all.15.parts_ref), custom_call_target="tpu_custom_call" | custom-call | tf_op jit(solution)/shard_map/pallas_call | solution.py:431
Async XLA Ops:
  2.3 16.9 %copy-start.4 = (bf16[1,256,512]{2,1,0:T(8,128)(2,1)S(1)}, bf16[1,256,512]{2,1,0:T(8,128)(2,1)}, u32[]{:S(2)}) copy-start(bf16[1,256,512]{2,1,0:T(8,128)(2,1)} %param.10) | copy-start | bytes 786436
  2.3 16.9 %copy-start.5 = (bf16[1,256,512]{2,1,0:T(8,128)(2,1)S(1)}, bf16[1,256,512]{2,1,0:T(8,128)(2,1)}, u32[]{:S(2)}) copy-start(bf16[1,256,512]{2,1,0:T(8,128)(2,1)} %param.11) | copy-start | bytes 786436
  2.3 22.4 %all-to-all-start = ((bf16[16,16,512]{2,1,0:T(8,128)(2,1)}), bf16[16,16,512]{2,1,0:T(8,128)(2,1)S(1)}, u32[]{:S(2)}, u32[]{:S(2)}) async-start(bf16[16,16,512]{2,1,0:T(8,128)(2,1)} %shard_map.128), calls=%async_computation | async-start | bytes 524288 | tf_op jit(solution)/shard_map/all_to_all | solution.py:445
  18.5 0.7 %copy-start.6 = (s32[1,2048]{1,0:T(1,128)S(1)}, s32[1,2048]{1,0:T(1,128)}, u32[]{:S(2)}) copy-start(s32[1,2048]{1,0:T(1,128)} %constant.2.clone.slots_ref) | copy-start | bytes 24580
  19.1 0.7 %copy-start.7 = (s32[512]{0:T(512)S(1)}, s32[512]{0:T(512)}, u32[]{:S(2)}) copy-start(s32[512]{0:T(512)} %group_hbm.1) | copy-start | bytes 6148
  19.8 1.2 %copy-start = (bf16[1,256,2048]{2,1,0:T(8,128)(2,1)S(1)}, bf16[1,256,2048]{2,1,0:T(8,128)(2,1)}, u32[]{:S(2)}) copy-start(bf16[1,256,2048]{2,1,0:T(8,128)(2,1)} %param.9) | copy-start | bytes 3145732
  21.1 1.2 %copy-start.2 = (bf16[1,256,2048]{2,1,0:T(8,128)(2,1)S(1)}, bf16[1,256,2048]{2,1,0:T(8,128)(2,1)}, u32[]{:S(2)}) copy-start(bf16[1,256,2048]{2,1,0:T(8,128)(2,1)} %param.14) | copy-start | bytes 3145732
  22.3 2.4 %copy-start.1 = (bf16[1,256,2048]{2,1,0:T(8,128)(2,1)S(1)}, bf16[1,256,2048]{2,1,0:T(8,128)(2,1)}, u32[]{:S(2)}) copy-start(bf16[1,256,2048]{2,1,0:T(8,128)(2,1)} %param.9) | copy-start | bytes 3145732
  22.3 2.4 %copy-start.3 = (bf16[1,256,2048]{2,1,0:T(8,128)(2,1)S(1)}, bf16[1,256,2048]{2,1,0:T(8,128)(2,1)}, u32[]{:S(2)}) copy-start(bf16[1,256,2048]{2,1,0:T(8,128)(2,1)} %param.14) | copy-start | bytes 3145732
  27.2 23.7 %all-to-all-start.1 = ((bf16[256,4,128]{2,1,0:T(4,128)(2,1)}), bf16[256,4,128]{2,1,0:T(4,128)(2,1)S(1)}, u32[]{:S(2)}, u32[]{:S(2)}) async-start(bf16[256,4,128]{2,1,0:T(4,128)(2,1)} %bitcast.8), calls=%async_computation.1 | async-start | bytes 524288 | tf_op jit(solution)/shard_map/all_to_all | solution.py:445
